TPU v7x, 32 devices: a whole 2x2x4 slice. The times are simulated.
32 devices in a mesh: wide: 16 (over z, y, x), narrow: 2 (over core).
Axes of the slice: x: 2, y: 2, z: 4, core: 2. Of those that a mesh axis runs over, the one named last changes fastest.
Arguments:
- integrals: bfloat16 [32, 6, 256, 1024], P(('wide', 'narrow')), may hold values from -1 to 1
- amplitudes: bfloat16 [32, 6, 256, 512], P(('wide', 'narrow')), may hold values from -6 to 6
- tile_count: int32 [32], P(('wide', 'narrow')), may hold values from 1 to 6, as said below
- row_orbitals: int32 [1024, 2], P(('wide', 'narrow')), may hold values from 0 to 575
- virtual_energy: float32 [576], replicated, may hold values from 0.2 to 3
- occupied_energy: float32 [512], replicated, may hold values from -3 to -0.8
- other_terms: float32 [1024, 512], P(('wide', 'narrow')), may hold values from -20 to 20
Outputs:
- update: float32 [1024, 512], P(('wide', 'narrow'))
- update_norm: float32 [], replicated
Inputs may be any that keep to these rules, and one draw needn't show every extreme that they name: A device's screened tiles are its first tile_count slots; some device holds 6 in every draw.
All inputs are finite; a program needn't handle non-finite values.
Results may differ from a plain program's by a relative error of at most 0.0003.
Values sent between devices are 32-bit elements; how exact they have to be, the bound alone decides.
No kernel may reach another device: no remote copies, remote signals or barrier semaphores. Data moves between devices by JAX's collectives and lax.ppermute only.
A program may use at most 64 MiB of HBM per device.

v0:
```python
import jax
import jax.numpy as jnp
from jax import lax
from jax.sharding import PartitionSpec as P


def add_slots(tile_block, amp_rows, lower, upper, row_total, running):
    tile_len = tile_block.shape[1]

    def add_tile(slot_index, partial_value):
        tile_one = lax.dynamic_slice(tile_block, (slot_index, 0, 0), (1, tile_len, row_total))[0]
        amp_one = lax.dynamic_index_in_dim(amp_rows, slot_index, 0, keepdims=False)
        return partial_value + lax.dot_general(
            tile_one, amp_one, (((0,), (0,)), ((), ())), preferred_element_type=jnp.float32
        )

    return lax.fori_loop(lower, upper, add_tile, running)


def shards(
    integrals, amplitudes, tile_count, row_orbitals, virtual_energy, occupied_energy, other_terms
):
    tile_block = integrals[0]
    amp_rows = amplitudes[0]
    live_count = tile_count[0]
    rows_all = tile_block.shape[2]
    width = amp_rows.shape[2]
    zero_index = jnp.int32(0)
    running = jnp.zeros(
        (lax.axis_size("wide") * (rows_all // lax.axis_size("wide")), width), jnp.float32
    )
    wide_rows = lax.psum_scatter(
        add_slots(
            tile_block,
            amp_rows,
            zero_index,
            live_count,
            lax.axis_size("wide") * (rows_all // lax.axis_size("wide")),
            running,
        ),
        "wide",
        scatter_dimension=0,
        tiled=True,
    )
    ladder = lax.psum_scatter(wide_rows, "narrow", scatter_dimension=0, tiled=True)
    orbital_ids = lax.broadcasted_iota(jnp.int32, (1, virtual_energy.shape[0]), 1)
    energy_row = virtual_energy[None, :]
    first_energy = jnp.sum(jnp.where(row_orbitals[:, 0:1] == orbital_ids, energy_row, 0.0), axis=1)
    second_energy = jnp.sum(jnp.where(row_orbitals[:, 1:2] == orbital_ids, energy_row, 0.0), axis=1)
    denominator = occupied_energy[None, :] - (first_energy + second_energy)[:, None]
    update = (ladder + other_terms) / denominator
    square_total = lax.psum(jnp.sum(update * update), ("wide", "narrow"))
    update_norm = jnp.sqrt(square_total / (rows_all * width))
    return (update, update_norm)


def solution(mesh):
    in_specs = (
        P(("wide", "narrow"), None, None, None),
        P(("wide", "narrow"), None, None, None),
        P(("wide", "narrow")),
        P(("wide", "narrow"), None),
        P(),
        P(),
        P(("wide", "narrow"), None),
    )
    out_specs = (P(("wide", "narrow"), None), P())
    return jax.shard_map(shards, mesh=mesh, in_specs=in_specs, out_specs=out_specs, check_vma=False)
```

profile of v0, /device:TPU:0, one launch (start us, length us, event | category | flops | bytes accessed | tf_op | source)
XLA Modules:
  0.0 164.8 jit_solution(15199393925118714662)
XLA Ops:
  7.2 0.0 reduce-scatter.3.cloned.1.call-start
  7.2 0.2 broadcast_in_dim.22
  7.5 5.2 %while.10 = (s32[]{:T(128)}, f32[1024,512]{1,0:T(8,128)S(1)}, s32[]{:T(128)}, bf16[6,256,1024]{2,1,0:T(8,128)(2,1)}, bf16[6,256,512]{2,1,0:T(8,128)(2,1)}, /*index=5*/s32[]{:T(128)}, s32[]{:T(128)}, s32[]{:T(128)}) while((s32[]{:T(128)}, f32[1024,512]{1,0:T(8,128)S(1)}, s32[]{:T(128)}, bf16[6,256,1024]{2,1,0:T(8,128)(2,1)}, ...), condition=%wide.region_1.2_spmd, body=%wide.region_0.1_spmd.sunk | while | flops 268959744 | bytes 4981887 | solution.py:17
  8.1 1.6 convolution_add_fusion.2
  10.4 1.6 convolution_add_fusion.2
  12.7 0.0 copy-start
  12.7 0.0 copy-start.4
  12.7 0.0 copy-start.2
  12.7 0.0 copy-start.1
  12.7 0.0 copy-start.3
  12.7 1.3 copy-done
  14.0 0.0 reduce-scatter.3.cloned.1.call-update
  14.0 0.0 reduce-scatter.5.cloned.1.call-start
  14.1 92.4 %reduce-scatter.3.cloned.1.call-done = f32[64,512]{1,0:T(8,128)} async-done(((f32[1024,512]{1,0:T(8,128)}), f32[64,512]{1,0:T(8,128)}) %reduce-scatter.3.cloned.1.call-update) | async-done | bytes 131088 | tf_op jit(solution)/shard_map/reduce_scatter | solution.py:32
  106.5 0.0 reduce-scatter.5.cloned.1.call-update
  106.5 0.0 copy-done.4
  106.6 0.0 copy-done.2
  106.6 0.2 select_reduce_fusion
  106.8 6.5 %reduce-scatter.5.cloned.1.call-done = f32[32,512]{1,0:T(8,128)} async-done(((f32[64,512]{1,0:T(8,128)}), f32[32,512]{1,0:T(8,128)}) %reduce-scatter.5.cloned.1.call-update) | async-done | bytes 65552 | tf_op jit(solution)/shard_map/reduce_scatter | solution.py:45
  113.3 0.0 copy-done.1
  113.3 0.0 copy-done.3
  113.3 2.2 %multiply_reduce_fusion = (f32[]{:T(128)}, f32[32,512]{1,0:T(8,128)}) fusion(f32[32]{0:T(128)S(1)} %add.28, f32[512]{0:T(512)S(1)} %copy-done.3, f32[32,512]{1,0:T(8,128)} %reduce-scatter.5.cloned.1.call-done, f32[32,512]{1,0:T(8,128)S(1)} %copy-done.1), kind=kLoop, calls=%fused_computation.10 | loop fusion | flops 81919 | bytes 198788 | tf_op jit(solution)/shard_map/reduce_sum | solution.py:52
  115.4 40.7 %psum.7 = f32[]{:T(128)} all-reduce(f32[]{:T(128)} %get-tuple-element.43), channel_id=1, replica_groups=mesh['wide'=16,'narrow'=2] {'wide','narrow'}, use_global_device_ids=true, to_apply=%region_7.8 | all-reduce | flops 1 | bytes 8 | tf_op jit(solution)/shard_map/psum | solution.py:52
  (2 shorter events, 0.0 us)
Async XLA Ops:
  7.2 99.4 %reduce-scatter.3.cloned.1.call-start = ((), (), s32[]{:S(2)}) async-start(), calls=%async_computation.2 | async-start | bytes 2228224 | tf_op jit(solution)/shard_map/reduce_scatter | solution.py:32
  12.7 1.4 copy-start
  12.7 93.9 %copy-start.4 = (s32[32,2]{0,1:T(2,128)S(1)}, s32[32,2]{0,1:T(2,128)}, u32[]{:S(2)}) copy-start(s32[32,2]{0,1:T(2,128)} %param.12) | copy-start | bytes 772
  12.7 93.9 %copy-start.2 = (f32[576]{0:T(1024)S(1)}, f32[576]{0:T(1024)}, u32[]{:S(2)}) copy-start(f32[576]{0:T(1024)} %param.13) | copy-start | bytes 6916
  12.7 100.6 %copy-start.1 = (f32[32,512]{1,0:T(8,128)S(1)}, f32[32,512]{1,0:T(8,128)}, u32[]{:S(2)}) copy-start(f32[32,512]{1,0:T(8,128)} %param.15) | copy-start | bytes 196612
  12.7 100.6 %copy-start.3 = (f32[512]{0:T(512)S(1)}, f32[512]{0:T(512)}, u32[]{:S(2)}) copy-start(f32[512]{0:T(512)} %param.14) | copy-start | bytes 6148
  14.0 99.3 %reduce-scatter.5.cloned.1.call-start = ((), (), s32[]{:S(2)}) async-start(), calls=%async_computation.3 | async-start | bytes 196608 | tf_op jit(solution)/shard_map/reduce_scatter | solution.py:45
Sparse Core Ops, SparseCore 0:
  14.1 92.3 reduce-scatter.2
  108.7 4.5 reduce-scatter.4
where the time goes:
time: 165 us
  waiting for transfers between devices  99 us (60%)
  blocking collectives  40.7 us (25%)
  between operations  15.9 us (10%)
  matrix products  3.18 us (2%)
  other arithmetic  2.35 us (1%)
  loops' own time  2 us (1%)
    reduce_scatter x1, waiting for transfers between devices, shards(): lax.psum_scatter(add_slots(tile_block, amp_rows, zero_index, live_count,...  92.4 us
    psum x1, blocking collectives, shards(): square_total = lax.psum(jnp.sum(update * update), ('wide', 'narrow'))  40.7 us
    reduce_scatter x1, waiting for transfers between devices, shards(): lax.psum_scatter(wide_rows, 'narrow', scatter_dimension=0, tiled=True)  6.52 us
  transfers between devices with their start and end apart: 2, of which 2 were waited for; matrix products, arithmetic and copies ran while one was open for 0% of the time, Pallas kernels for 0%

commit v1 on v0

v1 whole, which is shorter than its diff:
```python
import functools
import jax
import jax.numpy as jnp
from jax import lax
from jax.experimental import pallas as pl
from jax.experimental.pallas import tpu as pltpu
from jax.sharding import PartitionSpec as P

AXES = ("wide", "narrow")
GROUPS = 3
ROW_CHUNK = 256


def bit_order(stream, wide_bits):
    low = list(range(wide_bits))
    if wide_bits >= 2 and stream == 1:
        low[0], low[1] = low[1], low[0]
    return low


def ladder_kernel(block_rows, orders, place_ref, count_ref, tiles_ref, amps_ref, *refs):
    streams = len(orders)
    outs = refs[:streams]
    tile_buf, amp_buf, total, tile_sem, amp_sem = refs[streams:]
    slots, _, rows = tile_buf.shape
    width = amp_buf.shape[2]
    part = width // streams
    live = count_ref[0]
    wide_me, narrow_me = place_ref[0], place_ref[1]

    def copies(slot):
        return (
            pltpu.make_async_copy(amps_ref.at[slot], amp_buf.at[slot], amp_sem.at[slot]),
            pltpu.make_async_copy(tiles_ref.at[slot], tile_buf.at[slot], tile_sem.at[slot]),
        )

    for slot in range(slots):
        for copy in copies(slot):
            copy.start()
    group = slots // GROUPS
    for first in range(0, slots, group):
        members = range(first, first + group)
        for slot in members:
            for copy in copies(slot):
                copy.wait()
        amps = jnp.concatenate(
            [jnp.where(slot < live, amp_buf[slot], jnp.zeros_like(amp_buf[slot])) for slot in members], 0
        )
        for start in range(0, rows, ROW_CHUNK):
            tiles = jnp.concatenate([tile_buf[slot, :, start : start + ROW_CHUNK] for slot in members], 0)
            term = lax.dot_general(tiles, amps, (((0,), (0,)), ((), ())), preferred_element_type=jnp.float32)
            if first:
                term += total[start : start + ROW_CHUNK]
            if first + group < slots:
                total[start : start + ROW_CHUNK] = term
                continue
            for offset in range(0, ROW_CHUNK, block_rows):
                owner = (start + offset) // block_rows
                apart = (owner // 2) ^ wide_me
                cross = (owner % 2) ^ narrow_me
                for stream, order in enumerate(orders):
                    spot = cross
                    for bit in order:
                        spot = spot * 2 + ((apart >> bit) & 1)
                    where = pl.ds(pl.multiple_of(spot * block_rows, block_rows), block_rows)
                    outs[stream][where, :] = term[offset : offset + block_rows, stream * part : (stream + 1) * part]


def flip(value, axis, size, bits):
    return lax.ppermute(value, axis, [(i, i ^ bits) for i in range(size)])


def fast_ladder(tile_block, amp_rows, tile_count, wide, narrow):
    slots, depth, rows = tile_block.shape
    width = amp_rows.shape[2]
    block_rows = rows // (wide * narrow)
    wide_bits = wide.bit_length() - 1
    orders = [bit_order(stream, wide_bits) for stream in range(2)]
    part = width // 2
    place = jnp.stack([lax.axis_index("wide"), lax.axis_index("narrow")]).astype(jnp.int32)
    streams = pl.pallas_call(
        functools.partial(ladder_kernel, block_rows, orders),
        out_shape=[jax.ShapeDtypeStruct((rows, part), jnp.float32)] * 2,
        in_specs=[pl.BlockSpec(memory_space=pltpu.SMEM)] * 2 + [pl.BlockSpec(memory_space=pltpu.HBM)] * 2,
        out_specs=[pl.BlockSpec(memory_space=pltpu.VMEM)] * 2,
        scratch_shapes=[
            pltpu.VMEM((slots, depth, rows), tile_block.dtype),
            pltpu.VMEM((slots, depth, width), amp_rows.dtype),
            pltpu.VMEM((rows, width), jnp.float32),
            pltpu.SemaphoreType.DMA((slots,)),
            pltpu.SemaphoreType.DMA((slots,)),
        ],
        compiler_params=pltpu.CompilerParams(vmem_limit_bytes=32 << 20),
        cost_estimate=pl.CostEstimate(
            flops=2 * slots * depth * rows * width,
            bytes_accessed=2 * slots * depth * (rows + width) + 4 * rows * width,
            transcendentals=0,
        ),
    )(place, tile_count, tile_block, amp_rows)
    half = rows // 2
    streams = [s[:half] + flip(s[half:], "narrow", narrow, 1) for s in streams]
    for step in range(2):
        half //= 2
        streams = [
            s[:half] + flip(s[half:], "wide", wide, 1 << order[step]) for s, order in zip(streams, orders)
        ]
    joined = jnp.concatenate(streams, axis=1)
    ladder = joined[:block_rows]
    rest = orders[0][2:]
    for spot in range(1, 1 << len(rest)):
        bits = 0
        for index, bit in enumerate(rest):
            if (spot >> (len(rest) - 1 - index)) & 1:
                bits |= 1 << bit
        ladder += flip(joined[spot * block_rows : (spot + 1) * block_rows], "wide", wide, bits)
    return ladder


def plain_ladder(tile_block, amp_rows, tile_count):
    slots, depth, rows = tile_block.shape
    live = lax.broadcasted_iota(jnp.int32, (slots, 1, 1), 0) < tile_count[0]
    amps = jnp.where(live, amp_rows, jnp.zeros_like(amp_rows))
    partial = lax.dot_general(
        tile_block.reshape(slots * depth, rows),
        amps.reshape(slots * depth, amp_rows.shape[2]),
        (((0,), (0,)), ((), ())),
        preferred_element_type=jnp.float32,
    )
    partial = lax.psum_scatter(partial, "wide", scatter_dimension=0, tiled=True)
    return lax.psum_scatter(partial, "narrow", scatter_dimension=0, tiled=True)


def shards(wide, narrow, integrals, amplitudes, tile_count, row_orbitals, virtual_energy, occupied_energy, other_terms):
    tile_block = integrals[0]
    amp_rows = amplitudes[0]
    rows = tile_block.shape[2]
    width = amp_rows.shape[2]
    devices = wide * narrow
    fast = narrow == 2 and wide >= 4 and wide & (wide - 1) == 0 and rows % (16 * devices) == 0
    if fast:
        ladder = fast_ladder(tile_block, amp_rows, tile_count, wide, narrow)
    else:
        ladder = plain_ladder(tile_block, amp_rows, tile_count)
    orbital_ids = lax.broadcasted_iota(jnp.int32, (1, virtual_energy.shape[0]), 1)
    energy_row = virtual_energy[None, :]
    first_energy = jnp.sum(jnp.where(row_orbitals[:, 0:1] == orbital_ids, energy_row, 0.0), axis=1)
    second_energy = jnp.sum(jnp.where(row_orbitals[:, 1:2] == orbital_ids, energy_row, 0.0), axis=1)
    denominator = occupied_energy[None, :] - (first_energy + second_energy)[:, None]
    update = (ladder + other_terms) / denominator
    square = jnp.sum(update * update)
    if fast:
        every = lax.all_to_all(jnp.full((devices, 128), square), AXES, 0, 0, tiled=True)
        square_total = jnp.sum(every[:, 0])
    else:
        square_total = lax.psum(square, AXES)
    update_norm = jnp.sqrt(square_total / (rows * width))
    return (update, update_norm)


def solution(mesh):
    in_specs = (P(AXES, None, None, None), P(AXES, None, None, None), P(AXES), P(AXES, None), P(), P(), P(AXES, None))
    out_specs = (P(AXES, None), P())
    body = functools.partial(shards, mesh.shape["wide"], mesh.shape["narrow"])
    return jax.shard_map(body, mesh=mesh, in_specs=in_specs, out_specs=out_specs, check_vma=False)
```

time: 165 us -> 50.5 us (0.31)
  waiting for transfers between devices: 99 us -> 15.4 us
  blocking collectives: 40.7 us -> 9.11 us
  starting transfers between devices: 0.08 us -> 13 us
  between operations: 15.9 us -> 3.24 us
  matrix products: 3.18 us -> 0 us
  Pallas kernels: 0 us -> 3.05 us
  local copies, waits for them, and re-layouts: 1.58 us -> 4.11 us
  loops' own time: 2 us -> 0 us
    reduce_scatter x2 -> x0, waiting for transfers between devices: 99 us -> none  [the longest x1 92.4 us: shards(): lax.psum_scatter(add_slots(tile_block, amp_rows, zero_index, live_count,...]
    psum x1 -> x0, blocking collectives: 40.7 us -> none  [shards(): square_total = lax.psum(jnp.sum(update * update), ('wide', 'narrow'))]
    ppermute x0 -> x9, waiting for transfers between devices: none -> 15.4 us  [flip(): return lax.ppermute(value, axis, [(i, i ^ bits) for i in range(size)])]
    ppermute x0 -> x9, starting transfers between devices: none -> 13 us  [flip(): return lax.ppermute(value, axis, [(i, i ^ bits) for i in range(size)])]
    all_to_all x0 -> x1, blocking collectives: none -> 9.11 us  [shards(): lax.all_to_all(jnp.full((devices, 128), square), AXES, 0, 0, tiled=True)]
    dot_general x2 -> x0, matrix products: 3.18 us -> none  [add_tile(): lax.dot_general(tile_one, amp_one, (((0,), (0,)), ((), ())), preferred_el...]
    pallas_call x0 -> x1, Pallas kernels: none -> 3.05 us  [fast_ladder(): pl.pallas_call(functools.partial(ladder_kernel, block_rows, orders), out_...]
    unnamed x10 -> x12, local copies, waits for them, and re-layouts: 1.32 us -> 3.32 us
  transfers between devices with their start and end apart: 2 -> 9, of which waited for: 2 -> 7; matrix products, arithmetic and copies ran while one was open for 0% -> 1% of each run, Pallas kernels for 0% -> 0%
where the time goes in v1:
time: 50.5 us; the launch traced here: 50.3 us
  waiting for transfers between devices  15.4 us (30%)
  starting transfers between devices  13 us (26%)
  blocking collectives  9.11 us (18%)
  local copies, waits for them, and re-layouts  4.11 us (8%)
  between operations  3.24 us (6%)
  Pallas kernels  3.05 us (6%)
  other arithmetic  2.44 us (5%)
    ppermute x9, waiting for transfers between devices, flip(): return lax.ppermute(value, axis, [(i, i ^ bits) for i in range(size)])  15.4 us
    ppermute x9, starting transfers between devices, flip(): return lax.ppermute(value, axis, [(i, i ^ bits) for i in range(size)])  13 us
    all_to_all x1, blocking collectives, shards(): lax.all_to_all(jnp.full((devices, 128), square), AXES, 0, 0, tiled=True)  9.11 us
    unnamed x12, local copies, waits for them, and re-layouts  3.32 us
    pallas_call x1, Pallas kernels, fast_ladder(): pl.pallas_call(functools.partial(ladder_kernel, block_rows, orders), out_...  3.05 us
    reduce_sum x1, other arithmetic, shards(): square = jnp.sum(update * update)  1.31 us
  transfers between devices with their start and end apart: 9, of which 7 were waited for; matrix products, arithmetic and copies ran while one was open for 1% of the time, Pallas kernels for 0%

profile of v1, /device:TPU:0, one launch (start us, length us, event | category | flops | bytes accessed | tf_op | source)
XLA Modules:
  0.0 50.3 jit_solution(7991852627180036628)
XLA Ops:
  1.3 0.1 pad_add_fusion.place_ref
  1.4 0.0 copy-start
  1.4 1.9 %copy-done = bf16[1,6,256,1024]{3,2,1,0:T(8,128)(2,1)S(1)} copy-done((bf16[1,6,256,1024]{3,2,1,0:T(8,128)(2,1)S(1)}, bf16[1,6,256,1024]{3,2,1,0:T(8,128)(2,1)}, u32[]{:S(2)}) %copy-start) | copy-done | bytes 3145752
  3.2 0.0 copy-start.1
  3.2 1.4 %copy-done.1 = bf16[1,6,256,512]{3,2,1,0:T(8,128)(2,1)S(1)} copy-done((bf16[1,6,256,512]{3,2,1,0:T(8,128)(2,1)S(1)}, bf16[1,6,256,512]{3,2,1,0:T(8,128)(2,1)}, u32[]{:S(2)}) %copy-start.1) | copy-done | bytes 1572888
  4.7 3.1 %shard_map.86 = (f32[1024,256]{1,0:T(8,128)S(1)}, f32[1024,256]{1,0:T(8,128)S(1)}) custom-call(s32[2]{0:T(128)S(1)} %pad_add_fusion.place_ref, s32[1]{0:T(128)S(6)} %copy.11.count_ref, bf16[6,256,1024]{2,1,0:T(8,128)(2,1)S(1)} %bitcast.9, bf16[6,256,512]{2,1,0:T(8,128)(2,1)S(1)} %bitcast.10), custom_call_target="tpu_custom_call" | custom-call | flops 1610612736 | bytes 6815744 | tf_op jit(solution)/shard_map/pallas_call | solution.py:81
  7.7 0.0 copy-start.5
  7.8 0.5 %collective-permute-start.3 = (f32[512,256]{1,0:T(8,128)S(1)}, f32[512,256]{1,0:T(8,128)S(1)}, u32[]{:S(2)}, u32[]{:S(2)}) collective-permute-start(f32[512,256]{1,0:T(8,128)S(1)} %slice.64), channel_id=1, source_target_pairs={{0,1},{1,0},{2,3},{3,2},{4,5},{5,4},{6,7},{7,6},{8,9},{9,8},{10,11... | collective-permute-start | bytes 1572872 | tf_op jit(solution)/shard_map/ppermute | solution.py:70
  8.3 0.1 collective-permute-start
  8.4 1.4 %collective-permute-done.3 = f32[512,256]{1,0:T(8,128)S(1)} collective-permute-done((f32[512,256]{1,0:T(8,128)S(1)}, f32[512,256]{1,0:T(8,128)S(1)}, u32[]{:S(2)}, u32[]{:S(2)}) %collective-permute-start.3) | collective-permute-done | bytes 524320 | tf_op jit(solution)/shard_map/ppermute | solution.py:70
  9.8 0.1 slice_add_fusion
  9.9 0.0 copy-start.3
  9.9 0.0 copy-start.2
  9.9 0.0 copy-start.4
  10.0 3.0 %collective-permute-start.4 = (f32[256,256]{1,0:T(8,128)S(1)}, f32[256,256]{1,0:T(8,128)S(1)}, u32[]{:S(2)}, u32[]{:S(2)}) collective-permute-start(f32[256,256]{1,0:T(8,128)S(1)} %slice.81), channel_id=1, source_target_pairs={{0,4},{2,6},{4,0},{6,2},{8,12},{10,14},{12,8},{14,10},{16,20},{18,... | collective-permute-start | bytes 786440 | tf_op jit(solution)/shard_map/ppermute | solution.py:70
  12.9 0.0 collective-permute-done
  12.9 0.1 slice_add_fusion.1
  13.0 1.6 %collective-permute-start.1 = (f32[256,256]{1,0:T(8,128)S(1)}, f32[256,256]{1,0:T(8,128)S(1)}, u32[]{:S(2)}, u32[]{:S(2)}) collective-permute-start(f32[256,256]{1,0:T(8,128)S(1)} %slice.77), channel_id=1, source_target_pairs={{0,2},{2,0},{4,6},{6,4},{8,10},{10,8},{12,14},{14,12},{16,18},{18,... | collective-permute-start | bytes 786440 | tf_op jit(solution)/shard_map/ppermute | solution.py:70
  14.6 0.0 copy-done.5
  14.6 4.9 %collective-permute-done.4 = f32[256,256]{1,0:T(8,128)S(1)} collective-permute-done((f32[256,256]{1,0:T(8,128)S(1)}, f32[256,256]{1,0:T(8,128)S(1)}, u32[]{:S(2)}, u32[]{:S(2)}) %collective-permute-start.4) | collective-permute-done | bytes 262176 | tf_op jit(solution)/shard_map/ppermute | solution.py:70
  19.6 1.8 %collective-permute-start.5 = (f32[128,256]{1,0:T(8,128)S(1)}, f32[128,256]{1,0:T(8,128)S(1)}, u32[]{:S(2)}, u32[]{:S(2)}) collective-permute-start(f32[128,256]{1,0:T(8,128)S(1)} %slice.83), channel_id=1, source_target_pairs={{0,2},{2,0},{4,6},{6,4},{8,10},{10,8},{12,14},{14,12},{16,18},{18,... | collective-permute-start | bytes 393224 | tf_op jit(solution)/shard_map/ppermute | solution.py:70
  21.4 0.0 collective-permute-done.1
  21.4 1.6 %collective-permute-start.2 = (f32[128,256]{1,0:T(8,128)S(1)}, f32[128,256]{1,0:T(8,128)S(1)}, u32[]{:S(2)}, u32[]{:S(2)}) collective-permute-start(f32[128,256]{1,0:T(8,128)S(1)} %slice.79), channel_id=1, source_target_pairs={{0,4},{2,6},{4,0},{6,2},{8,12},{10,14},{12,8},{14,10},{16,20},{18,... | collective-permute-start | bytes 393224 | tf_op jit(solution)/shard_map/ppermute | solution.py:70
  23.0 1.7 %collective-permute-done.5 = f32[128,256]{1,0:T(8,128)S(1)} collective-permute-done((f32[128,256]{1,0:T(8,128)S(1)}, f32[128,256]{1,0:T(8,128)S(1)}, u32[]{:S(2)}, u32[]{:S(2)}) %collective-permute-start.5) | collective-permute-done | bytes 131104 | tf_op jit(solution)/shard_map/ppermute | solution.py:70
  24.7 1.8 %collective-permute-done.2 = f32[128,256]{1,0:T(8,128)S(1)} collective-permute-done((f32[128,256]{1,0:T(8,128)S(1)}, f32[128,256]{1,0:T(8,128)S(1)}, u32[]{:S(2)}, u32[]{:S(2)}) %collective-permute-start.2) | collective-permute-done | bytes 131104 | tf_op jit(solution)/shard_map/ppermute | solution.py:70
  26.5 2.7 %collective-permute-start.6 = (f32[32,512]{1,0:T(8,128)S(1)}, f32[32,512]{1,0:T(8,128)S(1)}, u32[]{:S(2)}, u32[]{:S(2)}) collective-permute-start(f32[32,512]{1,0:T(8,128)S(1)} %get-tuple-element.10), channel_id=1, source_target_pairs={{0,16},{2,18},{4,20},{6,22},{8,24},{10,26},{12,28},{14,30},{16,0},... | collective-permute-start | bytes 196616 | tf_op jit(solution)/shard_map/ppermute | solution.py:70
  29.1 1.6 %collective-permute-start.7 = (f32[32,512]{1,0:T(8,128)S(1)}, f32[32,512]{1,0:T(8,128)S(1)}, u32[]{:S(2)}, u32[]{:S(2)}) collective-permute-start(f32[32,512]{1,0:T(8,128)S(1)} %get-tuple-element.12), channel_id=1, source_target_pairs={{0,8},{2,10},{4,12},{6,14},{8,0},{10,2},{12,4},{14,6},{16,24},{18,... | collective-permute-start | bytes 196616 | tf_op jit(solution)/shard_map/ppermute | solution.py:70
  30.7 0.2 collective-permute-start.8
  30.9 0.0 copy-done.3
  30.9 0.2 select_reduce_fusion
  31.1 2.1 %collective-permute-done.6 = f32[32,512]{1,0:T(8,128)S(1)} collective-permute-done((f32[32,512]{1,0:T(8,128)S(1)}, f32[32,512]{1,0:T(8,128)S(1)}, u32[]{:S(2)}, u32[]{:S(2)}) %collective-permute-start.6) | collective-permute-done | bytes 65568 | tf_op jit(solution)/shard_map/ppermute | solution.py:70
  33.2 1.0 %collective-permute-done.7 = f32[32,512]{1,0:T(8,128)S(1)} collective-permute-done((f32[32,512]{1,0:T(8,128)S(1)}, f32[32,512]{1,0:T(8,128)S(1)}, u32[]{:S(2)}, u32[]{:S(2)}) %collective-permute-start.7) | collective-permute-done | bytes 65568 | tf_op jit(solution)/shard_map/ppermute | solution.py:70
  34.2 2.6 %collective-permute-done.8 = f32[32,512]{1,0:T(8,128)S(1)} collective-permute-done((f32[32,512]{1,0:T(8,128)S(1)}, f32[32,512]{1,0:T(8,128)S(1)}, u32[]{:S(2)}, u32[]{:S(2)}) %collective-permute-start.8) | collective-permute-done | bytes 65568 | tf_op jit(solution)/shard_map/ppermute | solution.py:70
  36.8 0.0 copy-done.2
  36.8 0.0 copy-done.4
  36.8 1.3 %multiply_reduce_fusion = (f32[]{:T(128)}, f32[32,512]{1,0:T(8,128)}) fusion(f32[32]{0:T(128)S(1)} %add.47, f32[512]{0:T(512)S(1)} %copy-done.4, f32[32,512]{1,0:T(8,128)S(1)} %copy-done.2, f32[32,512]{1,0:T(8,128)S(1)} %collective-permute-done.8, f32[32,512]{1,0:T(8,128)S(1)} %collective-permute-done.7, f32[32,512]{1,0:T(8,128)S(1)} %collective-permute-done.6, ...), kind=kLoop, calls=%fused_computation.25 | loop fusion | flops 147455 | bytes 592004 | tf_op jit(solution)/shard_map/reduce_sum | solution.py:150
  38.1 0.7 %broadcast_in_dim.24 = f32[32,1,128]{2,1,0:T(1,128)S(1)} broadcast(f32[]{:T(128)} %get-tuple-element.8), dimensions={} | broadcast | bytes 16388 | tf_op jit(solution)/shard_map/broadcast_in_dim | solution.py:152
  38.8 9.1 %all_to_all.9 = f32[32,1,128]{2,1,0:T(1,128)S(1)} all-to-all(f32[32,1,128]{2,1,0:T(1,128)S(1)} %broadcast_in_dim.24), channel_id=1, replica_groups=mesh['wide'=16,'narrow'=2] {'wide','narrow'}, dimensions={0} | all-to-all | bytes 32768 | tf_op jit(solution)/shard_map/all_to_all | solution.py:152
  47.9 0.6 %slice_reduce_fusion = f32[]{:T(128)} fusion(f32[32,128]{1,0:T(8,128)S(1)} %bitcast.11), kind=kLoop, calls=%fused_computation.26 | loop fusion | flops 31 | bytes 132 | tf_op jit(solution)/shard_map/reduce_sum | solution.py:153
  (13 shorter events, 0.3 us)
Async XLA Ops:
  1.4 1.9 %copy-start = (bf16[1,6,256,1024]{3,2,1,0:T(8,128)(2,1)S(1)}, bf16[1,6,256,1024]{3,2,1,0:T(8,128)(2,1)}, u32[]{:S(2)}) copy-start(bf16[1,6,256,1024]{3,2,1,0:T(8,128)(2,1)} %param.7) | copy-start | bytes 9437188
  3.2 1.4 %copy-start.1 = (bf16[1,6,256,512]{3,2,1,0:T(8,128)(2,1)S(1)}, bf16[1,6,256,512]{3,2,1,0:T(8,128)(2,1)}, u32[]{:S(2)}) copy-start(bf16[1,6,256,512]{3,2,1,0:T(8,128)(2,1)} %param.8) | copy-start | bytes 4718596
  7.7 6.9 %copy-start.5 = (s32[32,2]{0,1:T(2,128)S(1)}, s32[32,2]{0,1:T(2,128)}, u32[]{:S(2)}) copy-start(s32[32,2]{0,1:T(2,128)} %param.10) | copy-start | bytes 772
  7.8 2.1 %collective-permute-start.3 = (f32[512,256]{1,0:T(8,128)S(1)}, f32[512,256]{1,0:T(8,128)S(1)}, u32[]{:S(2)}, u32[]{:S(2)}) collective-permute-start(f32[512,256]{1,0:T(8,128)S(1)} %slice.64), channel_id=1, source_target_pairs={{0,1},{1,0},{2,3},{3,2},{4,5},{5,4},{6,7},{7,6},{8,9},{9,8},{10,11... | collective-permute-start | bytes 1572872 | tf_op jit(solution)/shard_map/ppermute | solution.py:70
  8.3 4.6 %collective-permute-start = (f32[512,256]{1,0:T(8,128)S(1)}, f32[512,256]{1,0:T(8,128)S(1)}, u32[]{:S(2)}, u32[]{:S(2)}) collective-permute-start(f32[512,256]{1,0:T(8,128)S(1)} %slice.58), channel_id=1, source_target_pairs={{0,1},{1,0},{2,3},{3,2},{4,5},{5,4},{6,7},{7,6},{8,9},{9,8},{10,11... | collective-permute-start | bytes 1572872 | tf_op jit(solution)/shard_map/ppermute | solution.py:70
  9.9 21.0 %copy-start.3 = (f32[576]{0:T(1024)S(1)}, f32[576]{0:T(1024)}, u32[]{:S(2)}) copy-start(f32[576]{0:T(1024)} %param.11) | copy-start | bytes 6916
  9.9 26.9 %copy-start.2 = (f32[32,512]{1,0:T(8,128)S(1)}, f32[32,512]{1,0:T(8,128)}, u32[]{:S(2)}) copy-start(f32[32,512]{1,0:T(8,128)} %param.13) | copy-start | bytes 196612
  9.9 26.9 %copy-start.4 = (f32[512]{0:T(512)S(1)}, f32[512]{0:T(512)}, u32[]{:S(2)}) copy-start(f32[512]{0:T(512)} %param.12) | copy-start | bytes 6148
  10.0 9.6 %collective-permute-start.4 = (f32[256,256]{1,0:T(8,128)S(1)}, f32[256,256]{1,0:T(8,128)S(1)}, u32[]{:S(2)}, u32[]{:S(2)}) collective-permute-start(f32[256,256]{1,0:T(8,128)S(1)} %slice.81), channel_id=1, source_target_pairs={{0,4},{2,6},{4,0},{6,2},{8,12},{10,14},{12,8},{14,10},{16,20},{18,... | collective-permute-start | bytes 786440 | tf_op jit(solution)/shard_map/ppermute | solution.py:70
  13.0 8.3 %collective-permute-start.1 = (f32[256,256]{1,0:T(8,128)S(1)}, f32[256,256]{1,0:T(8,128)S(1)}, u32[]{:S(2)}, u32[]{:S(2)}) collective-permute-start(f32[256,256]{1,0:T(8,128)S(1)} %slice.77), channel_id=1, source_target_pairs={{0,2},{2,0},{4,6},{6,4},{8,10},{10,8},{12,14},{14,12},{16,18},{18,... | collective-permute-start | bytes 786440 | tf_op jit(solution)/shard_map/ppermute | solution.py:70
  19.6 5.1 %collective-permute-start.5 = (f32[128,256]{1,0:T(8,128)S(1)}, f32[128,256]{1,0:T(8,128)S(1)}, u32[]{:S(2)}, u32[]{:S(2)}) collective-permute-start(f32[128,256]{1,0:T(8,128)S(1)} %slice.83), channel_id=1, source_target_pairs={{0,2},{2,0},{4,6},{6,4},{8,10},{10,8},{12,14},{14,12},{16,18},{18,... | collective-permute-start | bytes 393224 | tf_op jit(solution)/shard_map/ppermute | solution.py:70
  21.4 5.0 %collective-permute-start.2 = (f32[128,256]{1,0:T(8,128)S(1)}, f32[128,256]{1,0:T(8,128)S(1)}, u32[]{:S(2)}, u32[]{:S(2)}) collective-permute-start(f32[128,256]{1,0:T(8,128)S(1)} %slice.79), channel_id=1, source_target_pairs={{0,4},{2,6},{4,0},{6,2},{8,12},{10,14},{12,8},{14,10},{16,20},{18,... | collective-permute-start | bytes 393224 | tf_op jit(solution)/shard_map/ppermute | solution.py:70
  26.5 6.8 %collective-permute-start.6 = (f32[32,512]{1,0:T(8,128)S(1)}, f32[32,512]{1,0:T(8,128)S(1)}, u32[]{:S(2)}, u32[]{:S(2)}) collective-permute-start(f32[32,512]{1,0:T(8,128)S(1)} %get-tuple-element.10), channel_id=1, source_target_pairs={{0,16},{2,18},{4,20},{6,22},{8,24},{10,26},{12,28},{14,30},{16,0},... | collective-permute-start | bytes 196616 | tf_op jit(solution)/shard_map/ppermute | solution.py:70
  29.1 5.1 %collective-permute-start.7 = (f32[32,512]{1,0:T(8,128)S(1)}, f32[32,512]{1,0:T(8,128)S(1)}, u32[]{:S(2)}, u32[]{:S(2)}) collective-permute-start(f32[32,512]{1,0:T(8,128)S(1)} %get-tuple-element.12), channel_id=1, source_target_pairs={{0,8},{2,10},{4,12},{6,14},{8,0},{10,2},{12,4},{14,6},{16,24},{18,... | collective-permute-start | bytes 196616 | tf_op jit(solution)/shard_map/ppermute | solution.py:70
  30.7 6.1 %collective-permute-start.8 = (f32[32,512]{1,0:T(8,128)S(1)}, f32[32,512]{1,0:T(8,128)S(1)}, u32[]{:S(2)}, u32[]{:S(2)}) collective-permute-start(f32[32,512]{1,0:T(8,128)S(1)} %get-tuple-element.11), channel_id=1, source_target_pairs={{0,24},{2,26},{4,28},{6,30},{8,16},{10,18},{12,20},{14,22},{16,8},... | collective-permute-start | bytes 196616 | tf_op jit(solution)/shard_map/ppermute | solution.py:70

commit v2 on v1

v2 whole, which is shorter than its diff:
```python
import functools
import jax
import jax.numpy as jnp
from jax import lax
from jax.experimental import pallas as pl
from jax.experimental.pallas import tpu as pltpu
from jax.sharding import PartitionSpec as P

AXES = ("wide", "narrow")
ROW_CHUNK = 256
PLAN = ((0, 2, (0, 1), (1, 0)), (2, 4, (0, 1), (1, 0)))
SPOTS = (3, 2, 1)
STATIC = False


def ladder_kernel(block_rows, orders, bounds, place_ref, count_ref, tiles_ref, amps_ref, *refs):
    outs = refs[: len(bounds)]
    tile_buf, amp_buf, total, tile_sem, amp_sem = refs[len(bounds) :]
    slots, _, rows = tile_buf.shape
    live = count_ref[0]
    wide_me, narrow_me = place_ref[0], place_ref[1]

    def copies(slot):
        return (
            pltpu.make_async_copy(amps_ref.at[slot], amp_buf.at[slot], amp_sem.at[slot]),
            pltpu.make_async_copy(tiles_ref.at[slot], tile_buf.at[slot], tile_sem.at[slot]),
        )

    for slot in range(slots):

        def load_slot(slot=slot):
            for copy in copies(slot):
                copy.start()

        if slot and not STATIC:
            pl.when(slot < live)(load_slot)
        else:
            load_slot()
    def store(start, term, fresh):
        for offset in range(0, ROW_CHUNK, block_rows):
            owner = (start + offset) // block_rows
            apart = (owner // 2) ^ wide_me
            for piece, (low, high) in enumerate(bounds):
                spot = (owner % 2) ^ narrow_me
                for bit in orders[owner % 2][piece]:
                    spot = spot * 2 + ((apart >> bit) & 1)
                where = pl.ds(pl.multiple_of(spot * block_rows, block_rows), block_rows)
                block = term[offset : offset + block_rows, low:high]
                outs[piece][where, :] = block if fresh else outs[piece][where, :] + block

    if STATIC:
        group = 2
        for first in range(0, slots, group):
            members = range(first, first + group)
            for slot in members:
                for copy in copies(slot):
                    copy.wait()
            amps = jnp.concatenate(
                [jnp.where(slot < live, amp_buf[slot], jnp.zeros_like(amp_buf[slot])) for slot in members], 0
            )
            for start in range(0, rows, ROW_CHUNK):
                tiles = jnp.concatenate([tile_buf[slot, :, start : start + ROW_CHUNK] for slot in members], 0)
                term = lax.dot_general(tiles, amps, (((0,), (0,)), ((), ())), preferred_element_type=jnp.float32)
                if first:
                    term += total[start : start + ROW_CHUNK]
                if first + group < slots:
                    total[start : start + ROW_CHUNK] = term
                else:
                    store(start, term, True)
        return
    for slot in range(slots):

        def add_slot(slot=slot):
            for copy in copies(slot):
                copy.wait()
            for start in range(0, rows, ROW_CHUNK):
                term = lax.dot_general(
                    tile_buf[slot, :, start : start + ROW_CHUNK],
                    amp_buf[slot],
                    (((0,), (0,)), ((), ())),
                    preferred_element_type=jnp.float32,
                )
                store(start, term, slot == 0)

        if slot:
            pl.when(slot < live)(add_slot)
        else:
            add_slot()


def update_kernel(count, *refs):
    parts = refs[:count]
    other_ref, energy_ref, occupied_ref, update_ref, square_ref = refs[count:]
    ladder = parts[0][...]
    for part in parts[1:]:
        ladder += part[...]
    update = (ladder + other_ref[...]) / (occupied_ref[...] - energy_ref[...])
    update_ref[...] = update
    square_ref[...] = jnp.full(square_ref.shape, jnp.sum(update * update))


def norm_kernel(entries, squares_ref, norm_ref):
    total = jnp.sum(squares_ref[...], axis=0, keepdims=True)
    norm_ref[...] = jnp.sqrt(total / entries)[:, :1]


def flip(value, devices, masks):
    pairs = [(i, i ^ (2 * masks[i % 2])) for i in range(devices)]
    return lax.ppermute(value, AXES, pairs)


def fast_ladder(tile_block, amp_rows, tile_count, wide, narrow):
    slots, depth, rows = tile_block.shape
    width = amp_rows.shape[2]
    devices = wide * narrow
    block_rows = rows // devices
    rest = tuple(range(2, wide.bit_length() - 1))
    orders = [[plan[2 + core] + rest for plan in PLAN] for core in range(2)]
    bounds = [(plan[0] * width // 4, plan[1] * width // 4) for plan in PLAN]
    place = jnp.stack([lax.axis_index("wide"), lax.axis_index("narrow")]).astype(jnp.int32)
    pieces = pl.pallas_call(
        functools.partial(ladder_kernel, block_rows, orders, bounds),
        out_shape=[pltpu.VMEM((rows, high - low), jnp.float32) for low, high in bounds],
        in_specs=[pl.BlockSpec(memory_space=pltpu.SMEM)] * 2 + [pl.BlockSpec(memory_space=pltpu.HBM)] * 2,
        out_specs=[pl.BlockSpec(memory_space=pltpu.VMEM)] * len(bounds),
        scratch_shapes=[
            pltpu.VMEM((slots, depth, rows), tile_block.dtype),
            pltpu.VMEM((slots, depth, width), amp_rows.dtype),
            pltpu.VMEM((rows, width), jnp.float32),
            pltpu.SemaphoreType.DMA((slots,)),
            pltpu.SemaphoreType.DMA((slots,)),
        ],
        compiler_params=pltpu.CompilerParams(vmem_limit_bytes=32 << 20),
    )(
        place,
        tile_count,
        pltpu.with_memory_space_constraint(tile_block, pltpu.HBM),
        pltpu.with_memory_space_constraint(amp_rows, pltpu.HBM),
    )
    half = rows // 2
    swap = [(i, i ^ 1) for i in range(devices)]
    pieces = [s[:half] + lax.ppermute(s[half:], AXES, swap) for s in pieces]
    for step in range(2):
        half //= 2
        masks = [[1 << order[piece][step] for order in orders] for piece in range(len(pieces))]
        pieces = [s[:half] + flip(s[half:], devices, mask) for s, mask in zip(pieces, masks)]
    joined = jnp.concatenate(pieces, axis=1)
    parts = [joined[:block_rows]]
    for spot in SPOTS:
        mask = sum(1 << bit for i, bit in enumerate(rest) if (spot >> (len(rest) - 1 - i)) & 1)
        parts.append(flip(joined[spot * block_rows : (spot + 1) * block_rows], devices, [mask] * 2))
    return parts


def plain_ladder(tile_block, amp_rows, tile_count):
    slots, depth, rows = tile_block.shape
    live = lax.broadcasted_iota(jnp.int32, (slots, 1, 1), 0) < tile_count[0]
    amps = jnp.where(live, amp_rows, jnp.zeros_like(amp_rows))
    partial = lax.dot_general(
        tile_block.reshape(slots * depth, rows),
        amps.reshape(slots * depth, amp_rows.shape[2]),
        (((0,), (0,)), ((), ())),
        preferred_element_type=jnp.float32,
    )
    partial = lax.psum_scatter(partial, "wide", scatter_dimension=0, tiled=True)
    return lax.psum_scatter(partial, "narrow", scatter_dimension=0, tiled=True)


def shards(wide, narrow, integrals, amplitudes, tile_count, row_orbitals, virtual_energy, occupied_energy, other_terms):
    tile_block = integrals[0]
    amp_rows = amplitudes[0]
    rows = tile_block.shape[2]
    width = amp_rows.shape[2]
    devices = wide * narrow
    fast = narrow == 2 and wide >= 16 and wide & (wide - 1) == 0 and rows % (16 * devices) == 0 and width % 512 == 0
    orbital_ids = lax.broadcasted_iota(jnp.int32, (1, virtual_energy.shape[0]), 1)
    energy_row = virtual_energy[None, :]
    first_energy = jnp.sum(jnp.where(row_orbitals[:, 0:1] == orbital_ids, energy_row, 0.0), axis=1)
    second_energy = jnp.sum(jnp.where(row_orbitals[:, 1:2] == orbital_ids, energy_row, 0.0), axis=1)
    virtual_sum = (first_energy + second_energy)[:, None]
    occupied = occupied_energy[None, :]
    if fast:
        parts = fast_ladder(tile_block, amp_rows, tile_count, wide, narrow)
        update, squares = pl.pallas_call(
            functools.partial(update_kernel, len(parts)),
            out_shape=[
                jax.ShapeDtypeStruct(other_terms.shape, jnp.float32),
                pltpu.VMEM((devices, 128), jnp.float32),
            ],
            compiler_params=pltpu.CompilerParams(vmem_limit_bytes=4 << 20),
        )(*parts, other_terms, virtual_sum, occupied)
        squares = lax.all_to_all(squares, AXES, 0, 0, tiled=True)
        update_norm = pl.pallas_call(
            functools.partial(norm_kernel, rows * width),
            out_shape=jax.ShapeDtypeStruct((1, 1), jnp.float32),
            compiler_params=pltpu.CompilerParams(vmem_limit_bytes=4 << 20),
        )(squares).reshape(())
    else:
        ladder = plain_ladder(tile_block, amp_rows, tile_count)
        update = (ladder + other_terms) / (occupied - virtual_sum)
        update_norm = jnp.sqrt(lax.psum(jnp.sum(update * update), AXES) / (rows * width))
    return (update, update_norm)


def solution(mesh):
    in_specs = (P(AXES, None, None, None), P(AXES, None, None, None), P(AXES), P(AXES, None), P(), P(), P(AXES, None))
    out_specs = (P(AXES, None), P())
    body = functools.partial(shards, mesh.shape["wide"], mesh.shape["narrow"])
    return jax.shard_map(body, mesh=mesh, in_specs=in_specs, out_specs=out_specs, check_vma=False)
```

time: 50.5 us -> 45.2 us (0.90)
  local copies, waits for them, and re-layouts: 4.11 us -> 0.25 us
  blocking collectives: 9.11 us -> 11.1 us
  other arithmetic: 2.44 us -> 0.52 us
  between operations: 3.24 us -> 1.4 us
  starting transfers between devices: 13 us -> 11.2 us
  waiting for transfers between devices: 15.4 us -> 17.2 us
    unnamed x12 -> x8, local copies, waits for them, and re-layouts: 3.32 us -> 0.02 us
    all_to_all x1, blocking collectives: 9.11 us -> 11.1 us  [shards(): squares = lax.all_to_all(squares, AXES, 0, 0, tiled=True)]
    reduce_sum x2 -> x0, other arithmetic: 1.91 us -> none  [the longest x1 1.31 us: shards(): square = jnp.sum(update * update)]
    ppermute x9, waiting for transfers between devices: 15.4 us -> 17.2 us  [the longest x7 15.7 us: flip(): return lax.ppermute(value, AXES, pairs)]
    ppermute x9, starting transfers between devices: 13 us -> 11.2 us  [the longest x7 8.16 us: flip(): return lax.ppermute(value, AXES, pairs)]
    broadcast_in_dim x1 -> x0, local copies, waits for them, and re-layouts: 0.65 us -> none  [shards(): jnp.full((devices, 128), square)]
    pallas_call x1 -> x3, Pallas kernels: 3.05 us -> 3.48 us  [the longest x1 2.24 us: fast_ladder(): pl.pallas_call(functools.partial(ladder_kernel, block_rows, orders, bound...]
  transfers between devices with their start and end apart: 9 -> 9, of which waited for: 7 -> 9; matrix products, arithmetic and copies ran while one was open for 1% -> 1% of each run, Pallas kernels for 0% -> 0%
where the time goes in v2:
time: 45.2 us; the launch traced here: 45.1 us
  waiting for transfers between devices  17.2 us (38%)
  starting transfers between devices  11.2 us (25%)
  blocking collectives  11.1 us (25%)
  Pallas kernels  3.48 us (8%)
  between operations  1.4 us (3%)
  other arithmetic  0.52 us (1%)
    ppermute x7, waiting for transfers between devices, flip(): return lax.ppermute(value, AXES, pairs)  15.7 us
    all_to_all x1, blocking collectives, shards(): squares = lax.all_to_all(squares, AXES, 0, 0, tiled=True)  11.1 us
    ppermute x7, starting transfers between devices, flip(): return lax.ppermute(value, AXES, pairs)  8.16 us
    ppermute x2, starting transfers between devices, fast_ladder(): pieces = [s[:half] + lax.ppermute(s[half:], AXES, swap) for s in pieces]  3.04 us
    pallas_call x1, Pallas kernels, fast_ladder(): pl.pallas_call(functools.partial(ladder_kernel, block_rows, orders, bound...  2.24 us
    ppermute x2, waiting for transfers between devices, fast_ladder(): pieces = [s[:half] + lax.ppermute(s[half:], AXES, swap) for s in pieces]  1.54 us
  transfers between devices with their start and end apart: 9, of which 9 were waited for; matrix products, arithmetic and copies ran while one was open for 1% of the time, Pallas kernels for 0%

profile of v2, /device:TPU:0, one launch (start us, length us, event | category | flops | bytes accessed | tf_op | source)
XLA Modules:
  0.0 45.1 jit_solution(12388830472913552800)
XLA Ops:
  1.3 0.1 pad_add_fusion.place_ref
  1.4 0.0 copy-start.3
  1.4 2.2 %shard_map.86 = (f32[1024,256]{1,0:T(8,128)S(1)}, f32[1024,256]{1,0:T(8,128)S(1)}) custom-call(s32[2]{0:T(128)S(1)} %pad_add_fusion.place_ref, s32[1]{0:T(128)S(6)} %copy.14.count_ref, bf16[6,256,1024]{2,1,0:T(8,128)(2,1)} %bitcast.19, bf16[6,256,512]{2,1,0:T(8,128)(2,1)} %bitcast.20), custom_call_target="tpu_custom_call" | custom-call | tf_op jit(solution)/shard_map/pallas_call | solution.py:121
  3.6 0.0 copy-start.2
  3.7 3.0 %collective-permute-start = (f32[512,256]{1,0:T(8,128)S(1)}, f32[512,256]{1,0:T(8,128)S(1)}, u32[]{:S(2)}, u32[]{:S(2)}) collective-permute-start(f32[512,256]{1,0:T(8,128)S(1)} %slice.55), channel_id=1, source_target_pairs={{0,1},{1,0},{2,3},{3,2},{4,5},{5,4},{6,7},{7,6},{8,9},{9,8},{10,11... | collective-permute-start | bytes 1572872 | tf_op jit(solution)/shard_map/ppermute | solution.py:142
  6.7 0.1 collective-permute-start.3
  6.7 0.0 copy-done.3
  6.8 1.4 %collective-permute-done = f32[512,256]{1,0:T(8,128)S(1)} collective-permute-done((f32[512,256]{1,0:T(8,128)S(1)}, f32[512,256]{1,0:T(8,128)S(1)}, u32[]{:S(2)}, u32[]{:S(2)}) %collective-permute-start) | collective-permute-done | bytes 524320 | tf_op jit(solution)/shard_map/ppermute | solution.py:142
  8.2 0.1 slice_add_fusion.1
  8.2 0.0 copy-start
  8.2 0.0 copy-start.1
  8.3 0.5 %collective-permute-start.1 = (f32[256,256]{1,0:T(8,128)S(1)}, f32[256,256]{1,0:T(8,128)S(1)}, u32[]{:S(2)}, u32[]{:S(2)}) collective-permute-start(f32[256,256]{1,0:T(8,128)S(1)} %slice.73), channel_id=1, source_target_pairs={{0,2},{1,5},{2,0},{3,7},{4,6},{5,1},{6,4},{7,3},{8,10},{9,13},{10,... | collective-permute-start | bytes 786440 | tf_op jit(solution)/shard_map/ppermute | solution.py:109
  8.8 0.1 collective-permute-done.3
  8.9 0.1 slice_add_fusion
  9.0 1.5 %collective-permute-start.4 = (f32[256,256]{1,0:T(8,128)S(1)}, f32[256,256]{1,0:T(8,128)S(1)}, u32[]{:S(2)}, u32[]{:S(2)}) collective-permute-start(f32[256,256]{1,0:T(8,128)S(1)} %slice.77), channel_id=1, source_target_pairs={{0,2},{1,5},{2,0},{3,7},{4,6},{5,1},{6,4},{7,3},{8,10},{9,13},{10,... | collective-permute-start | bytes 786440 | tf_op jit(solution)/shard_map/ppermute | solution.py:109
  10.5 0.0 copy-done.2
  10.5 0.2 select_reduce_fusion
  10.7 4.0 %collective-permute-done.1 = f32[256,256]{1,0:T(8,128)S(1)} collective-permute-done((f32[256,256]{1,0:T(8,128)S(1)}, f32[256,256]{1,0:T(8,128)S(1)}, u32[]{:S(2)}, u32[]{:S(2)}) %collective-permute-start.1) | collective-permute-done | bytes 262176 | tf_op jit(solution)/shard_map/ppermute | solution.py:109
  14.8 0.5 %collective-permute-start.2 = (f32[128,256]{1,0:T(8,128)S(1)}, f32[128,256]{1,0:T(8,128)S(1)}, u32[]{:S(2)}, u32[]{:S(2)}) collective-permute-start(f32[128,256]{1,0:T(8,128)S(1)} %slice.75), channel_id=1, source_target_pairs={{0,4},{1,3},{2,6},{3,1},{4,0},{5,7},{6,2},{7,5},{8,12},{9,11},{10,... | collective-permute-start | bytes 393224 | tf_op jit(solution)/shard_map/ppermute | solution.py:109
  15.3 2.7 %collective-permute-done.4 = f32[256,256]{1,0:T(8,128)S(1)} collective-permute-done((f32[256,256]{1,0:T(8,128)S(1)}, f32[256,256]{1,0:T(8,128)S(1)}, u32[]{:S(2)}, u32[]{:S(2)}) %collective-permute-start.4) | collective-permute-done | bytes 262176 | tf_op jit(solution)/shard_map/ppermute | solution.py:109
  18.1 0.5 %collective-permute-start.5 = (f32[128,256]{1,0:T(8,128)S(1)}, f32[128,256]{1,0:T(8,128)S(1)}, u32[]{:S(2)}, u32[]{:S(2)}) collective-permute-start(f32[128,256]{1,0:T(8,128)S(1)} %slice.79), channel_id=1, source_target_pairs={{0,4},{1,3},{2,6},{3,1},{4,0},{5,7},{6,2},{7,5},{8,12},{9,11},{10,... | collective-permute-start | bytes 393224 | tf_op jit(solution)/shard_map/ppermute | solution.py:109
  18.6 1.2 %collective-permute-done.2 = f32[128,256]{1,0:T(8,128)S(1)} collective-permute-done((f32[128,256]{1,0:T(8,128)S(1)}, f32[128,256]{1,0:T(8,128)S(1)}, u32[]{:S(2)}, u32[]{:S(2)}) %collective-permute-start.2) | collective-permute-done | bytes 131104 | tf_op jit(solution)/shard_map/ppermute | solution.py:109
  19.8 3.3 %collective-permute-done.5 = f32[128,256]{1,0:T(8,128)S(1)} collective-permute-done((f32[128,256]{1,0:T(8,128)S(1)}, f32[128,256]{1,0:T(8,128)S(1)}, u32[]{:S(2)}, u32[]{:S(2)}) %collective-permute-start.5) | collective-permute-done | bytes 131104 | tf_op jit(solution)/shard_map/ppermute | solution.py:109
  23.2 4.5 %collective-permute-start.6 = (f32[32,512]{1,0:T(8,128)S(1)}, f32[32,512]{1,0:T(8,128)S(1)}, u32[]{:S(2)}, u32[]{:S(2)}) collective-permute-start(f32[32,512]{1,0:T(8,128)S(1)} %get-tuple-element.14), channel_id=1, source_target_pairs={{0,24},{1,25},{2,26},{3,27},{4,28},{5,29},{6,30},{7,31},{8,16},{9,... | collective-permute-start | bytes 196616 | tf_op jit(solution)/shard_map/ppermute | solution.py:109
  27.6 0.0 collective-permute-start.7
  27.6 0.6 %collective-permute-start.8 = (f32[32,512]{1,0:T(8,128)S(1)}, f32[32,512]{1,0:T(8,128)S(1)}, u32[]{:S(2)}, u32[]{:S(2)}) collective-permute-start(f32[32,512]{1,0:T(8,128)S(1)} %get-tuple-element.12), channel_id=1, source_target_pairs={{0,16},{1,17},{2,18},{3,19},{4,20},{5,21},{6,22},{7,23},{8,24},{9,... | collective-permute-start | bytes 196616 | tf_op jit(solution)/shard_map/ppermute | solution.py:109
  28.3 0.1 copy.12.refs_5_
  28.4 1.6 %collective-permute-done.6.refs_1_ = f32[32,512]{1,0:T(8,128)S(1)} collective-permute-done((f32[32,512]{1,0:T(8,128)S(1)}, f32[32,512]{1,0:T(8,128)S(1)}, u32[]{:S(2)}, u32[]{:S(2)}) %collective-permute-start.6) | collective-permute-done | bytes 65568 | tf_op jit(solution)/shard_map/ppermute | solution.py:109
  30.0 1.9 %collective-permute-done.7.refs_2_ = f32[32,512]{1,0:T(8,128)S(1)} collective-permute-done((f32[32,512]{1,0:T(8,128)S(1)}, f32[32,512]{1,0:T(8,128)S(1)}, u32[]{:S(2)}, u32[]{:S(2)}) %collective-permute-start.7) | collective-permute-done | bytes 65568 | tf_op jit(solution)/shard_map/ppermute | solution.py:109
  31.9 0.9 %collective-permute-done.8.refs_3_ = f32[32,512]{1,0:T(8,128)S(1)} collective-permute-done((f32[32,512]{1,0:T(8,128)S(1)}, f32[32,512]{1,0:T(8,128)S(1)}, u32[]{:S(2)}, u32[]{:S(2)}) %collective-permute-start.8) | collective-permute-done | bytes 65568 | tf_op jit(solution)/shard_map/ppermute | solution.py:109
  32.8 0.0 copy-done
  32.8 0.0 copy-done.1
  32.8 0.7 %shard_map.87 = (f32[32,512]{1,0:T(8,128)}, f32[32,128]{1,0:T(8,128)S(1)}) custom-call(f32[32,512]{1,0:T(8,128)S(1)} %get-tuple-element.13.refs_0_, f32[32,512]{1,0:T(8,128)S(1)} %collective-permute-done.6.refs_1_, f32[32,512]{1,0:T(8,128)S(1)} %collective-permute-done.7.refs_2_, f32[32,512]{1,0:T(8,128)S(1)} %collective-permute-done.8.refs_3_, ...), custom_call_target="tpu_custom_call" | custom-call | tf_op jit(solution)/shard_map/pallas_call | solution.py:184
  33.5 11.1 %all_to_all.11 = f32[32,1,128]{2,1,0:T(1,128)S(1)} all-to-all(f32[32,1,128]{2,1,0:T(1,128)S(1)} %bitcast.17), channel_id=1, replica_groups=mesh['wide'=16,'narrow'=2] {'wide','narrow'}, dimensions={0} | all-to-all | bytes 32768 | tf_op jit(solution)/shard_map/all_to_all | solution.py:192
  44.6 0.5 %shard_map.88 = f32[1,1]{1,0:T(1,128)} custom-call(f32[32,128]{1,0:T(8,128)S(1)} %bitcast.16), custom_call_target="tpu_custom_call" | custom-call | tf_op jit(solution)/shard_map/pallas_call | solution.py:193
  (13 shorter events, 0.3 us)
Async XLA Ops:
  1.4 5.4 %copy-start.3 = (s32[32,2]{0,1:T(2,128)S(1)}, s32[32,2]{0,1:T(2,128)}, u32[]{:S(2)}) copy-start(s32[32,2]{0,1:T(2,128)} %param.10) | copy-start | bytes 772
  3.6 6.9 %copy-start.2 = (f32[576]{0:T(1024)S(1)}, f32[576]{0:T(1024)}, u32[]{:S(2)}) copy-start(f32[576]{0:T(1024)} %param.11) | copy-start | bytes 6916
  3.7 4.5 %collective-permute-start = (f32[512,256]{1,0:T(8,128)S(1)}, f32[512,256]{1,0:T(8,128)S(1)}, u32[]{:S(2)}, u32[]{:S(2)}) collective-permute-start(f32[512,256]{1,0:T(8,128)S(1)} %slice.55), channel_id=1, source_target_pairs={{0,1},{1,0},{2,3},{3,2},{4,5},{5,4},{6,7},{7,6},{8,9},{9,8},{10,11... | collective-permute-start | bytes 1572872 | tf_op jit(solution)/shard_map/ppermute | solution.py:142
  6.7 2.2 %collective-permute-start.3 = (f32[512,256]{1,0:T(8,128)S(1)}, f32[512,256]{1,0:T(8,128)S(1)}, u32[]{:S(2)}, u32[]{:S(2)}) collective-permute-start(f32[512,256]{1,0:T(8,128)S(1)} %slice.61), channel_id=1, source_target_pairs={{0,1},{1,0},{2,3},{3,2},{4,5},{5,4},{6,7},{7,6},{8,9},{9,8},{10,11... | collective-permute-start | bytes 1572872 | tf_op jit(solution)/shard_map/ppermute | solution.py:142
  8.2 24.6 %copy-start = (f32[32,512]{1,0:T(8,128)S(1)}, f32[32,512]{1,0:T(8,128)}, u32[]{:S(2)}) copy-start(f32[32,512]{1,0:T(8,128)} %refs_4_.1) | copy-start | bytes 196612
  8.2 24.6 %copy-start.1 = (f32[512]{0:T(512)S(1)}, f32[512]{0:T(512)}, u32[]{:S(2)}) copy-start(f32[512]{0:T(512)} %param.12) | copy-start | bytes 6148
  8.3 6.4 %collective-permute-start.1 = (f32[256,256]{1,0:T(8,128)S(1)}, f32[256,256]{1,0:T(8,128)S(1)}, u32[]{:S(2)}, u32[]{:S(2)}) collective-permute-start(f32[256,256]{1,0:T(8,128)S(1)} %slice.73), channel_id=1, source_target_pairs={{0,2},{1,5},{2,0},{3,7},{4,6},{5,1},{6,4},{7,3},{8,10},{9,13},{10,... | collective-permute-start | bytes 786440 | tf_op jit(solution)/shard_map/ppermute | solution.py:109
  9.0 9.0 %collective-permute-start.4 = (f32[256,256]{1,0:T(8,128)S(1)}, f32[256,256]{1,0:T(8,128)S(1)}, u32[]{:S(2)}, u32[]{:S(2)}) collective-permute-start(f32[256,256]{1,0:T(8,128)S(1)} %slice.77), channel_id=1, source_target_pairs={{0,2},{1,5},{2,0},{3,7},{4,6},{5,1},{6,4},{7,3},{8,10},{9,13},{10,... | collective-permute-start | bytes 786440 | tf_op jit(solution)/shard_map/ppermute | solution.py:109
  14.8 5.0 %collective-permute-start.2 = (f32[128,256]{1,0:T(8,128)S(1)}, f32[128,256]{1,0:T(8,128)S(1)}, u32[]{:S(2)}, u32[]{:S(2)}) collective-permute-start(f32[128,256]{1,0:T(8,128)S(1)} %slice.75), channel_id=1, source_target_pairs={{0,4},{1,3},{2,6},{3,1},{4,0},{5,7},{6,2},{7,5},{8,12},{9,11},{10,... | collective-permute-start | bytes 393224 | tf_op jit(solution)/shard_map/ppermute | solution.py:109
  18.1 5.0 %collective-permute-start.5 = (f32[128,256]{1,0:T(8,128)S(1)}, f32[128,256]{1,0:T(8,128)S(1)}, u32[]{:S(2)}, u32[]{:S(2)}) collective-permute-start(f32[128,256]{1,0:T(8,128)S(1)} %slice.79), channel_id=1, source_target_pairs={{0,4},{1,3},{2,6},{3,1},{4,0},{5,7},{6,2},{7,5},{8,12},{9,11},{10,... | collective-permute-start | bytes 393224 | tf_op jit(solution)/shard_map/ppermute | solution.py:109
  23.2 6.8 %collective-permute-start.6 = (f32[32,512]{1,0:T(8,128)S(1)}, f32[32,512]{1,0:T(8,128)S(1)}, u32[]{:S(2)}, u32[]{:S(2)}) collective-permute-start(f32[32,512]{1,0:T(8,128)S(1)} %get-tuple-element.14), channel_id=1, source_target_pairs={{0,24},{1,25},{2,26},{3,27},{4,28},{5,29},{6,30},{7,31},{8,16},{9,... | collective-permute-start | bytes 196616 | tf_op jit(solution)/shard_map/ppermute | solution.py:109
  27.6 4.3 %collective-permute-start.7 = (f32[32,512]{1,0:T(8,128)S(1)}, f32[32,512]{1,0:T(8,128)S(1)}, u32[]{:S(2)}, u32[]{:S(2)}) collective-permute-start(f32[32,512]{1,0:T(8,128)S(1)} %get-tuple-element.15), channel_id=1, source_target_pairs={{0,8},{1,9},{2,10},{3,11},{4,12},{5,13},{6,14},{7,15},{8,0},{9,1},... | collective-permute-start | bytes 196616 | tf_op jit(solution)/shard_map/ppermute | solution.py:109
  27.6 5.2 %collective-permute-start.8 = (f32[32,512]{1,0:T(8,128)S(1)}, f32[32,512]{1,0:T(8,128)S(1)}, u32[]{:S(2)}, u32[]{:S(2)}) collective-permute-start(f32[32,512]{1,0:T(8,128)S(1)} %get-tuple-element.12), channel_id=1, source_target_pairs={{0,16},{1,17},{2,18},{3,19},{4,20},{5,21},{6,22},{7,23},{8,24},{9,... | collective-permute-start | bytes 196616 | tf_op jit(solution)/shard_map/ppermute | solution.py:109

commit v3 on v2

--- a/solution.py
+++ b/solution.py
@@ -8,14 +8,17 @@
 
 AXES = ("wide", "narrow")
 ROW_CHUNK = 256
-PLAN = ((0, 2, (0, 1), (1, 0)), (2, 4, (0, 1), (1, 0)))
-SPOTS = (3, 2, 1)
-STATIC = False
+ROUTES = ((0, 1), (1, 0))
 
 
-def ladder_kernel(block_rows, orders, bounds, place_ref, count_ref, tiles_ref, amps_ref, *refs):
-    outs = refs[: len(bounds)]
-    tile_buf, amp_buf, total, tile_sem, amp_sem = refs[len(bounds) :]
+def position(order, wide_index):
+    spot = wide_index * 0
+    for bit in order:
+        spot = spot * 2 + ((wide_index >> bit) & 1)
+    return spot
+
+
+def ladder_kernel(block_rows, place_ref, count_ref, tiles_ref, amps_ref, out_ref, tile_buf, amp_buf, tile_sem, amp_sem):
     slots, _, rows = tile_buf.shape
     live = count_ref[0]
     wide_me, narrow_me = place_ref[0], place_ref[1]
@@ -32,60 +35,33 @@
             for copy in copies(slot):
                 copy.start()
 
-        if slot and not STATIC:
-            pl.when(slot < live)(load_slot)
-        else:
-            load_slot()
-    def store(start, term, fresh):
-        for offset in range(0, ROW_CHUNK, block_rows):
-            owner = (start + offset) // block_rows
-            apart = (owner // 2) ^ wide_me
-            for piece, (low, high) in enumerate(bounds):
-                spot = (owner % 2) ^ narrow_me
-                for bit in orders[owner % 2][piece]:
-                    spot = spot * 2 + ((apart >> bit) & 1)
-                where = pl.ds(pl.multiple_of(spot * block_rows, block_rows), block_rows)
-                block = term[offset : offset + block_rows, low:high]
-                outs[piece][where, :] = block if fresh else outs[piece][where, :] + block
+        pl.when(slot < live)(load_slot)
 
-    if STATIC:
-        group = 2
-        for first in range(0, slots, group):
-            members = range(first, first + group)
-            for slot in members:
-                for copy in copies(slot):
-                    copy.wait()
-            amps = jnp.concatenate(
-                [jnp.where(slot < live, amp_buf[slot], jnp.zeros_like(amp_buf[slot])) for slot in members], 0
-            )
-            for start in range(0, rows, ROW_CHUNK):
-                tiles = jnp.concatenate([tile_buf[slot, :, start : start + ROW_CHUNK] for slot in members], 0)
-                term = lax.dot_general(tiles, amps, (((0,), (0,)), ((), ())), preferred_element_type=jnp.float32)
-                if first:
-                    term += total[start : start + ROW_CHUNK]
-                if first + group < slots:
-                    total[start : start + ROW_CHUNK] = term
-                else:
-                    store(start, term, True)
-        return
-    for slot in range(slots):
+    def spot_of(wide, narrow, route):
+        return (wide >> 2) * 8 + narrow * 4 + position(route, wide & 3)
 
-        def add_slot(slot=slot):
+    mine = [spot_of(wide_me, narrow_me, route) for route in ROUTES]
+
+    def add_slots(members, fresh):
+        for slot in members:
             for copy in copies(slot):
                 copy.wait()
-            for start in range(0, rows, ROW_CHUNK):
-                term = lax.dot_general(
-                    tile_buf[slot, :, start : start + ROW_CHUNK],
-                    amp_buf[slot],
-                    (((0,), (0,)), ((), ())),
-                    preferred_element_type=jnp.float32,
-                )
-                store(start, term, slot == 0)
+        amps = jnp.concatenate([amp_buf[slot] for slot in members], 0)
+        for start in range(0, rows, ROW_CHUNK):
+            tiles = jnp.concatenate([tile_buf[slot, :, start : start + ROW_CHUNK] for slot in members], 0)
+            term = lax.dot_general(tiles, amps, (((0,), (0,)), ((), ())), preferred_element_type=jnp.float32)
+            for offset in range(0, ROW_CHUNK, block_rows):
+                wide, narrow = divmod((start + offset) // block_rows, 2)
+                spot = mine[narrow] ^ spot_of(wide, narrow, ROUTES[narrow])
+                where = pl.ds(pl.multiple_of(spot * block_rows, block_rows), block_rows)
+                block = term[offset : offset + block_rows]
+                out_ref[where, :] = block if fresh else out_ref[where, :] + block
 
-        if slot:
-            pl.when(slot < live)(add_slot)
-        else:
-            add_slot()
+    for first in range(0, slots, 2):
+        alone = (live == first + 1) if first + 1 < slots else (live > first)
+        pl.when(alone)(functools.partial(add_slots, [first], first == 0))
+        if first + 1 < slots:
+            pl.when(live > first + 1)(functools.partial(add_slots, [first, first + 1], first == 0))
 
 
 def update_kernel(count, *refs):
@@ -114,19 +90,15 @@
     width = amp_rows.shape[2]
     devices = wide * narrow
     block_rows = rows // devices
-    rest = tuple(range(2, wide.bit_length() - 1))
-    orders = [[plan[2 + core] + rest for plan in PLAN] for core in range(2)]
-    bounds = [(plan[0] * width // 4, plan[1] * width // 4) for plan in PLAN]
     place = jnp.stack([lax.axis_index("wide"), lax.axis_index("narrow")]).astype(jnp.int32)
-    pieces = pl.pallas_call(
-        functools.partial(ladder_kernel, block_rows, orders, bounds),
-        out_shape=[pltpu.VMEM((rows, high - low), jnp.float32) for low, high in bounds],
+    partial = pl.pallas_call(
+        functools.partial(ladder_kernel, block_rows),
+        out_shape=pltpu.VMEM((rows, width), jnp.float32),
         in_specs=[pl.BlockSpec(memory_space=pltpu.SMEM)] * 2 + [pl.BlockSpec(memory_space=pltpu.HBM)] * 2,
-        out_specs=[pl.BlockSpec(memory_space=pltpu.VMEM)] * len(bounds),
+        out_specs=pl.BlockSpec(memory_space=pltpu.VMEM),
         scratch_shapes=[
             pltpu.VMEM((slots, depth, rows), tile_block.dtype),
             pltpu.VMEM((slots, depth, width), amp_rows.dtype),
-            pltpu.VMEM((rows, width), jnp.float32),
             pltpu.SemaphoreType.DMA((slots,)),
             pltpu.SemaphoreType.DMA((slots,)),
         ],
@@ -137,18 +109,21 @@
         pltpu.with_memory_space_constraint(tile_block, pltpu.HBM),
         pltpu.with_memory_space_constraint(amp_rows, pltpu.HBM),
     )
-    half = rows // 2
+    far = wide // 4
+    partial = partial.reshape(far, 2, 4, block_rows, width)
     swap = [(i, i ^ 1) for i in range(devices)]
-    pieces = [s[:half] + lax.ppermute(s[half:], AXES, swap) for s in pieces]
+    groups = [range(far // 2), range(far // 2, far)]
+    pieces = [partial[g.start : g.stop] for g in groups]
+    pieces = [s[:, 0] + lax.ppermute(s[:, 1], AXES, swap) for s in pieces]
     for step in range(2):
-        half //= 2
-        masks = [[1 << order[piece][step] for order in orders] for piece in range(len(pieces))]
-        pieces = [s[:half] + flip(s[half:], devices, mask) for s, mask in zip(pieces, masks)]
-    joined = jnp.concatenate(pieces, axis=1)
-    parts = [joined[:block_rows]]
-    for spot in SPOTS:
-        mask = sum(1 << bit for i, bit in enumerate(rest) if (spot >> (len(rest) - 1 - i)) & 1)
-        parts.append(flip(joined[spot * block_rows : (spot + 1) * block_rows], devices, [mask] * 2))
+        half = 2 >> step
+        masks = [1 << route[step] for route in ROUTES]
+        pieces = [s[:, :half] + flip(s[:, half:], devices, masks) for s in pieces]
+    parts = []
+    for g, s in zip(groups, pieces):
+        for spot in g:
+            block = s[spot - g.start, 0]
+            parts.append(flip(block, devices, [4 * spot] * 2) if spot else block)
     return parts
 
 

time: 45.2 us -> 42.7 us (0.945)
  waiting for transfers between devices: 17.2 us -> 9.2 us
  starting transfers between devices: 11.2 us -> 14.8 us
  blocking collectives: 11.1 us -> 12.5 us
  Pallas kernels: 3.48 us -> 4.01 us
    ppermute x7, waiting for transfers between devices: 15.7 us -> 7.91 us  [flip(): return lax.ppermute(value, AXES, pairs)]
    ppermute x7, starting transfers between devices: 8.16 us -> 14.1 us  [flip(): return lax.ppermute(value, AXES, pairs)]
    ppermute x2, starting transfers between devices: 3.04 us -> 0.63 us  [fast_ladder(): pieces = [s[:, 0] + lax.ppermute(s[:, 1], AXES, swap) for s in pieces]]
    all_to_all x1, blocking collectives: 11.1 us -> 12.5 us  [shards(): squares = lax.all_to_all(squares, AXES, 0, 0, tiled=True)]
    pallas_call x1, Pallas kernels: 2.24 us -> 2.76 us  [fast_ladder(): pl.pallas_call(functools.partial(ladder_kernel, block_rows), out_shape=pl...]
  transfers between devices with their start and end apart: 9 -> 9, of which waited for: 9 -> 5; matrix products, arithmetic and copies ran while one was open for 1% -> 2% of each run, Pallas kernels for 0% -> 0%
where the time goes in v3:
time: 42.7 us; the launch traced here: 42.9 us
  starting transfers between devices  14.8 us (35%)
  blocking collectives  12.5 us (29%)
  waiting for transfers between devices  9.2 us (22%)
  Pallas kernels  4.01 us (9%)
  between operations  1.43 us (3%)
  other arithmetic  0.54 us (1%)
  local copies, waits for them, and re-layouts  0.44 us (1%)
    ppermute x7, starting transfers between devices, flip(): return lax.ppermute(value, AXES, pairs)  14.1 us
    all_to_all x1, blocking collectives, shards(): squares = lax.all_to_all(squares, AXES, 0, 0, tiled=True)  12.5 us
    ppermute x7, waiting for transfers between devices, flip(): return lax.ppermute(value, AXES, pairs)  7.91 us
    pallas_call x1, Pallas kernels, fast_ladder(): pl.pallas_call(functools.partial(ladder_kernel, block_rows), out_shape=pl...  2.76 us
    ppermute x2, waiting for transfers between devices, fast_ladder(): pieces = [s[:, 0] + lax.ppermute(s[:, 1], AXES, swap) for s in pieces]  1.29 us
  transfers between devices with their start and end apart: 9, of which 5 were waited for; matrix products, arithmetic and copies ran while one was open for 2% of the time, Pallas kernels for 0%

profile of v3, /device:TPU:0, one launch (start us, length us, event | category | flops | bytes accessed | tf_op | source)
XLA Modules:
  0.0 42.9 jit_solution(14548007028038939273)
XLA Ops:
  1.3 0.1 pad_add_fusion.place_ref
  1.4 2.8 %shard_map.86 = f32[1024,512]{1,0:T(8,128)S(1)} custom-call(s32[2]{0:T(128)S(1)} %pad_add_fusion.place_ref, s32[1]{0:T(128)S(6)} %copy.31.count_ref, bf16[6,256,1024]{2,1,0:T(8,128)(2,1)} %bitcast.53, bf16[6,256,512]{2,1,0:T(8,128)(2,1)} %bitcast.54), custom_call_target="tpu_custom_call" | custom-call | tf_op jit(solution)/shard_map/pallas_call | solution.py:94
  4.1 0.2 fusion.2
  4.3 0.0 copy-start.3
  4.4 0.1 collective-permute-start.4
  4.5 0.6 %collective-permute-start = (f32[2,4,32,512]{3,2,1,0:T(8,128)S(1)}, f32[2,4,32,512]{3,2,1,0:T(8,128)S(1)}, u32[]{:S(2)}, u32[]{:S(2)}) collective-permute-start(f32[2,4,32,512]{3,2,1,0:T(8,128)S(1)} %slice_bitcast_fusion.2), channel_id=1, source_target_pairs={{0,1},{1,0},{2,3},{3,2},{4,5},{5,4},{6,7},{7,6},{8,9},{9,8},{10,11... | collective-permute-start | bytes 1572872 | tf_op jit(solution)/shard_map/ppermute | solution.py:117
  5.0 0.0 copy-done.3
  5.0 0.0 copy-start.2
  5.1 1.3 %collective-permute-done.4 = f32[2,4,32,512]{3,2,1,0:T(8,128)S(1)} collective-permute-done((f32[2,4,32,512]{3,2,1,0:T(8,128)S(1)}, f32[2,4,32,512]{3,2,1,0:T(8,128)S(1)}, u32[]{:S(2)}, u32[]{:S(2)}) %collective-permute-start.4) | collective-permute-done | bytes 524320 | tf_op jit(solution)/shard_map/ppermute | solution.py:117
  6.3 0.1 fusion
  6.5 2.5 %collective-permute-start.5 = (f32[2,2,32,512]{3,2,1,0:T(8,128)S(1)}, f32[2,2,32,512]{3,2,1,0:T(8,128)S(1)}, u32[]{:S(2)}, u32[]{:S(2)}) collective-permute-start(f32[2,2,32,512]{3,2,1,0:T(8,128)S(1)} %slice.101), channel_id=1, source_target_pairs={{0,2},{1,5},{2,0},{3,7},{4,6},{5,1},{6,4},{7,3},{8,10},{9,13},{10,... | collective-permute-start | bytes 786440 | tf_op jit(solution)/shard_map/ppermute | solution.py:85
  8.9 0.0 collective-permute-done
  9.0 0.1 fusion.1
  9.0 0.0 copy-start
  9.1 0.0 copy-start.1
  9.1 0.6 %collective-permute-start.1 = (f32[2,2,32,512]{3,2,1,0:T(8,128)S(1)}, f32[2,2,32,512]{3,2,1,0:T(8,128)S(1)}, u32[]{:S(2)}, u32[]{:S(2)}) collective-permute-start(f32[2,2,32,512]{3,2,1,0:T(8,128)S(1)} %slice.92), channel_id=1, source_target_pairs={{0,2},{1,5},{2,0},{3,7},{4,6},{5,1},{6,4},{7,3},{8,10},{9,13},{10,... | collective-permute-start | bytes 786440 | tf_op jit(solution)/shard_map/ppermute | solution.py:85
  9.7 0.0 copy-done.2
  9.7 0.2 select_reduce_fusion
  9.9 3.4 %collective-permute-done.5 = f32[2,2,32,512]{3,2,1,0:T(8,128)S(1)} collective-permute-done((f32[2,2,32,512]{3,2,1,0:T(8,128)S(1)}, f32[2,2,32,512]{3,2,1,0:T(8,128)S(1)}, u32[]{:S(2)}, u32[]{:S(2)}) %collective-permute-start.5) | collective-permute-done | bytes 262176 | tf_op jit(solution)/shard_map/ppermute | solution.py:85
  13.4 2.6 %collective-permute-start.6 = (f32[2,1,32,512]{3,2,1,0:T(8,128)S(1)}, f32[2,1,32,512]{3,2,1,0:T(8,128)S(1)}, u32[]{:S(2)}, u32[]{:S(2)}) collective-permute-start(f32[2,1,32,512]{3,2,1,0:T(8,128)S(1)} %slice.103), channel_id=1, source_target_pairs={{0,4},{1,3},{2,6},{3,1},{4,0},{5,7},{6,2},{7,5},{8,12},{9,11},{10,... | collective-permute-start | bytes 393224 | tf_op jit(solution)/shard_map/ppermute | solution.py:85
  16.0 0.1 collective-permute-done.1
  16.2 3.4 %collective-permute-start.2 = (f32[2,1,32,512]{3,2,1,0:T(8,128)S(1)}, f32[2,1,32,512]{3,2,1,0:T(8,128)S(1)}, u32[]{:S(2)}, u32[]{:S(2)}) collective-permute-start(f32[2,1,32,512]{3,2,1,0:T(8,128)S(1)} %slice.94), channel_id=1, source_target_pairs={{0,4},{1,3},{2,6},{3,1},{4,0},{5,7},{6,2},{7,5},{8,12},{9,11},{10,... | collective-permute-start | bytes 393224 | tf_op jit(solution)/shard_map/ppermute | solution.py:85
  19.5 0.0 collective-permute-done.6
  19.6 3.4 %collective-permute-start.7 = (f32[32,512]{1,0:T(8,128)S(1)}, f32[32,512]{1,0:T(8,128)S(1)}, u32[]{:S(2)}, u32[]{:S(2)}) collective-permute-start(f32[32,512]{1,0:T(8,128)S(1)} %get-tuple-element.11), channel_id=1, source_target_pairs={{0,16},{1,17},{2,18},{3,19},{4,20},{5,21},{6,22},{7,23},{8,24},{9,... | collective-permute-start | bytes 196616 | tf_op jit(solution)/shard_map/ppermute | solution.py:85
  23.0 1.1 %collective-permute-start.8 = (f32[32,512]{1,0:T(8,128)S(1)}, f32[32,512]{1,0:T(8,128)S(1)}, u32[]{:S(2)}, u32[]{:S(2)}) collective-permute-start(f32[32,512]{1,0:T(8,128)S(1)} %get-tuple-element.10), channel_id=1, source_target_pairs={{0,24},{1,25},{2,26},{3,27},{4,28},{5,29},{6,30},{7,31},{8,16},{9,... | collective-permute-start | bytes 196616 | tf_op jit(solution)/shard_map/ppermute | solution.py:85
  24.0 0.0 collective-permute-done.2
  24.1 0.6 %collective-permute-start.3 = (f32[32,512]{1,0:T(8,128)S(1)}, f32[32,512]{1,0:T(8,128)S(1)}, u32[]{:S(2)}, u32[]{:S(2)}) collective-permute-start(f32[32,512]{1,0:T(8,128)S(1)} %get-tuple-element.12), channel_id=1, source_target_pairs={{0,8},{1,9},{2,10},{3,11},{4,12},{5,13},{6,14},{7,15},{8,0},{9,1},... | collective-permute-start | bytes 196616 | tf_op jit(solution)/shard_map/ppermute | solution.py:85
  24.7 0.1 copy.25.refs_5_
  24.7 0.9 %collective-permute-done.7.refs_2_ = f32[32,512]{1,0:T(8,128)S(1)} collective-permute-done((f32[32,512]{1,0:T(8,128)S(1)}, f32[32,512]{1,0:T(8,128)S(1)}, u32[]{:S(2)}, u32[]{:S(2)}) %collective-permute-start.7) | collective-permute-done | bytes 65568 | tf_op jit(solution)/shard_map/ppermute | solution.py:85
  25.6 3.5 %collective-permute-done.8.refs_3_ = f32[32,512]{1,0:T(8,128)S(1)} collective-permute-done((f32[32,512]{1,0:T(8,128)S(1)}, f32[32,512]{1,0:T(8,128)S(1)}, u32[]{:S(2)}, u32[]{:S(2)}) %collective-permute-start.8) | collective-permute-done | bytes 65568 | tf_op jit(solution)/shard_map/ppermute | solution.py:85
  29.1 0.0 collective-permute-done.3.refs_1_
  29.1 0.0 copy-done
  29.1 0.0 copy-done.1
  29.1 0.7 %shard_map.87 = (f32[32,512]{1,0:T(8,128)}, f32[32,128]{1,0:T(8,128)S(1)}) custom-call(f32[32,512]{1,0:T(8,128)S(1)} %get-tuple-element.13.refs_0_, f32[32,512]{1,0:T(8,128)S(1)} %collective-permute-done.3.refs_1_, f32[32,512]{1,0:T(8,128)S(1)} %collective-permute-done.7.refs_2_, f32[32,512]{1,0:T(8,128)S(1)} %collective-permute-done.8.refs_3_, ...), custom_call_target="tpu_custom_call" | custom-call | tf_op jit(solution)/shard_map/pallas_call | solution.py:159
  29.9 12.5 %all_to_all.11 = f32[32,1,128]{2,1,0:T(1,128)S(1)} all-to-all(f32[32,1,128]{2,1,0:T(1,128)S(1)} %bitcast.47), channel_id=1, replica_groups=mesh['wide'=16,'narrow'=2] {'wide','narrow'}, dimensions={0} | all-to-all | bytes 32768 | tf_op jit(solution)/shard_map/all_to_all | solution.py:167
  42.4 0.5 %shard_map.88 = f32[1,1]{1,0:T(1,128)} custom-call(f32[32,128]{1,0:T(8,128)S(1)} %bitcast.46), custom_call_target="tpu_custom_call" | custom-call | tf_op jit(solution)/shard_map/pallas_call | solution.py:168
  (14 shorter events, 0.3 us)
Async XLA Ops:
  4.3 0.7 %copy-start.3 = (s32[32,2]{0,1:T(2,128)S(1)}, s32[32,2]{0,1:T(2,128)}, u32[]{:S(2)}) copy-start(s32[32,2]{0,1:T(2,128)} %param.10) | copy-start | bytes 772
  4.4 2.0 %collective-permute-start.4 = (f32[2,4,32,512]{3,2,1,0:T(8,128)S(1)}, f32[2,4,32,512]{3,2,1,0:T(8,128)S(1)}, u32[]{:S(2)}, u32[]{:S(2)}) collective-permute-start(f32[2,4,32,512]{3,2,1,0:T(8,128)S(1)} %slice_bitcast_fusion), channel_id=1, source_target_pairs={{0,1},{1,0},{2,3},{3,2},{4,5},{5,4},{6,7},{7,6},{8,9},{9,8},{10,11... | collective-permute-start | bytes 1572872 | tf_op jit(solution)/shard_map/ppermute | solution.py:117
  4.5 4.5 %collective-permute-start = (f32[2,4,32,512]{3,2,1,0:T(8,128)S(1)}, f32[2,4,32,512]{3,2,1,0:T(8,128)S(1)}, u32[]{:S(2)}, u32[]{:S(2)}) collective-permute-start(f32[2,4,32,512]{3,2,1,0:T(8,128)S(1)} %slice_bitcast_fusion.2), channel_id=1, source_target_pairs={{0,1},{1,0},{2,3},{3,2},{4,5},{5,4},{6,7},{7,6},{8,9},{9,8},{10,11... | collective-permute-start | bytes 1572872 | tf_op jit(solution)/shard_map/ppermute | solution.py:117
  5.0 4.7 %copy-start.2 = (f32[576]{0:T(1024)S(1)}, f32[576]{0:T(1024)}, u32[]{:S(2)}) copy-start(f32[576]{0:T(1024)} %param.11) | copy-start | bytes 6916
  6.5 6.8 %collective-permute-start.5 = (f32[2,2,32,512]{3,2,1,0:T(8,128)S(1)}, f32[2,2,32,512]{3,2,1,0:T(8,128)S(1)}, u32[]{:S(2)}, u32[]{:S(2)}) collective-permute-start(f32[2,2,32,512]{3,2,1,0:T(8,128)S(1)} %slice.101), channel_id=1, source_target_pairs={{0,2},{1,5},{2,0},{3,7},{4,6},{5,1},{6,4},{7,3},{8,10},{9,13},{10,... | collective-permute-start | bytes 786440 | tf_op jit(solution)/shard_map/ppermute | solution.py:85
  9.0 20.1 %copy-start = (f32[32,512]{1,0:T(8,128)S(1)}, f32[32,512]{1,0:T(8,128)}, u32[]{:S(2)}) copy-start(f32[32,512]{1,0:T(8,128)} %refs_4_.1) | copy-start | bytes 196612
  9.1 20.1 %copy-start.1 = (f32[512]{0:T(512)S(1)}, f32[512]{0:T(512)}, u32[]{:S(2)}) copy-start(f32[512]{0:T(512)} %param.12) | copy-start | bytes 6148
  9.1 7.0 %collective-permute-start.1 = (f32[2,2,32,512]{3,2,1,0:T(8,128)S(1)}, f32[2,2,32,512]{3,2,1,0:T(8,128)S(1)}, u32[]{:S(2)}, u32[]{:S(2)}) collective-permute-start(f32[2,2,32,512]{3,2,1,0:T(8,128)S(1)} %slice.92), channel_id=1, source_target_pairs={{0,2},{1,5},{2,0},{3,7},{4,6},{5,1},{6,4},{7,3},{8,10},{9,13},{10,... | collective-permute-start | bytes 786440 | tf_op jit(solution)/shard_map/ppermute | solution.py:85
  13.4 6.2 %collective-permute-start.6 = (f32[2,1,32,512]{3,2,1,0:T(8,128)S(1)}, f32[2,1,32,512]{3,2,1,0:T(8,128)S(1)}, u32[]{:S(2)}, u32[]{:S(2)}) collective-permute-start(f32[2,1,32,512]{3,2,1,0:T(8,128)S(1)} %slice.103), channel_id=1, source_target_pairs={{0,4},{1,3},{2,6},{3,1},{4,0},{5,7},{6,2},{7,5},{8,12},{9,11},{10,... | collective-permute-start | bytes 393224 | tf_op jit(solution)/shard_map/ppermute | solution.py:85
  16.2 7.9 %collective-permute-start.2 = (f32[2,1,32,512]{3,2,1,0:T(8,128)S(1)}, f32[2,1,32,512]{3,2,1,0:T(8,128)S(1)}, u32[]{:S(2)}, u32[]{:S(2)}) collective-permute-start(f32[2,1,32,512]{3,2,1,0:T(8,128)S(1)} %slice.94), channel_id=1, source_target_pairs={{0,4},{1,3},{2,6},{3,1},{4,0},{5,7},{6,2},{7,5},{8,12},{9,11},{10,... | collective-permute-start | bytes 393224 | tf_op jit(solution)/shard_map/ppermute | solution.py:85
  19.6 6.0 %collective-permute-start.7 = (f32[32,512]{1,0:T(8,128)S(1)}, f32[32,512]{1,0:T(8,128)S(1)}, u32[]{:S(2)}, u32[]{:S(2)}) collective-permute-start(f32[32,512]{1,0:T(8,128)S(1)} %get-tuple-element.11), channel_id=1, source_target_pairs={{0,16},{1,17},{2,18},{3,19},{4,20},{5,21},{6,22},{7,23},{8,24},{9,... | collective-permute-start | bytes 196616 | tf_op jit(solution)/shard_map/ppermute | solution.py:85
  23.0 6.1 %collective-permute-start.8 = (f32[32,512]{1,0:T(8,128)S(1)}, f32[32,512]{1,0:T(8,128)S(1)}, u32[]{:S(2)}, u32[]{:S(2)}) collective-permute-start(f32[32,512]{1,0:T(8,128)S(1)} %get-tuple-element.10), channel_id=1, source_target_pairs={{0,24},{1,25},{2,26},{3,27},{4,28},{5,29},{6,30},{7,31},{8,16},{9,... | collective-permute-start | bytes 196616 | tf_op jit(solution)/shard_map/ppermute | solution.py:85
  24.1 5.0 %collective-permute-start.3 = (f32[32,512]{1,0:T(8,128)S(1)}, f32[32,512]{1,0:T(8,128)S(1)}, u32[]{:S(2)}, u32[]{:S(2)}) collective-permute-start(f32[32,512]{1,0:T(8,128)S(1)} %get-tuple-element.12), channel_id=1, source_target_pairs={{0,8},{1,9},{2,10},{3,11},{4,12},{5,13},{6,14},{7,15},{8,0},{9,1},... | collective-permute-start | bytes 196616 | tf_op jit(solution)/shard_map/ppermute | solution.py:85

commit v4 on v3

--- a/solution.py
+++ b/solution.py
@@ -8,7 +8,8 @@
 
 AXES = ("wide", "narrow")
 ROW_CHUNK = 256
-ROUTES = ((0, 1), (1, 0))
+FAR_ROUTES = ((0, 1), (1, 0))
+NEAR_ROUTES = ((2, 1, 0), (1, 0, 2))
 
 
 def position(order, wide_index):
@@ -18,7 +19,7 @@
     return spot
 
 
-def ladder_kernel(block_rows, place_ref, count_ref, tiles_ref, amps_ref, out_ref, tile_buf, amp_buf, tile_sem, amp_sem):
+def ladder_kernel(block_rows, planes, place_ref, count_ref, tiles_ref, amps_ref, out_ref, tile_buf, amp_buf, tile_sem, amp_sem):
     slots, _, rows = tile_buf.shape
     live = count_ref[0]
     wide_me, narrow_me = place_ref[0], place_ref[1]
@@ -37,10 +38,14 @@
 
         pl.when(slot < live)(load_slot)
 
-    def spot_of(wide, narrow, route):
-        return (wide >> 2) * 8 + narrow * 4 + position(route, wide & 3)
-
-    mine = [spot_of(wide_me, narrow_me, route) for route in ROUTES]
+    def spot_of(wide_index, narrow):
+        apart = wide_me ^ wide_index
+        cross = narrow_me ^ narrow
+        plane = apart >> 2
+        first, second, third = NEAR_ROUTES[narrow]
+        far_spot = plane * 8 + cross * 4 + position(FAR_ROUTES[narrow], apart)
+        near_spot = (plane >> 1) * 16 + position((third,), apart) * 8 + cross * 4 + position((first, second), apart)
+        return jnp.where(plane >= planes // 2, far_spot, near_spot)
 
     def add_slots(members, fresh):
         for slot in members:
@@ -52,7 +57,7 @@
             term = lax.dot_general(tiles, amps, (((0,), (0,)), ((), ())), preferred_element_type=jnp.float32)
             for offset in range(0, ROW_CHUNK, block_rows):
                 wide, narrow = divmod((start + offset) // block_rows, 2)
-                spot = mine[narrow] ^ spot_of(wide, narrow, ROUTES[narrow])
+                spot = spot_of(wide, narrow)
                 where = pl.ds(pl.multiple_of(spot * block_rows, block_rows), block_rows)
                 block = term[offset : offset + block_rows]
                 out_ref[where, :] = block if fresh else out_ref[where, :] + block
@@ -92,7 +97,7 @@
     block_rows = rows // devices
     place = jnp.stack([lax.axis_index("wide"), lax.axis_index("narrow")]).astype(jnp.int32)
     partial = pl.pallas_call(
-        functools.partial(ladder_kernel, block_rows),
+        functools.partial(ladder_kernel, block_rows, wide // 4),
         out_shape=pltpu.VMEM((rows, width), jnp.float32),
         in_specs=[pl.BlockSpec(memory_space=pltpu.SMEM)] * 2 + [pl.BlockSpec(memory_space=pltpu.HBM)] * 2,
         out_specs=pl.BlockSpec(memory_space=pltpu.VMEM),
@@ -117,13 +122,16 @@
     pieces = [s[:, 0] + lax.ppermute(s[:, 1], AXES, swap) for s in pieces]
     for step in range(2):
         half = 2 >> step
-        masks = [1 << route[step] for route in ROUTES]
-        pieces = [s[:, :half] + flip(s[:, half:], devices, masks) for s in pieces]
+        masks = [[1 << route[step] for route in routes] for routes in (NEAR_ROUTES, FAR_ROUTES)]
+        pieces = [s[:, :half] + flip(s[:, half:], devices, mask) for s, mask in zip(pieces, masks)]
     parts = []
     for g, s in zip(groups, pieces):
         for spot in g:
             block = s[spot - g.start, 0]
-            parts.append(flip(block, devices, [4 * spot] * 2) if spot else block)
+            masks = [4 * spot] * 2
+            if spot < far // 2:
+                masks = [(4 * spot & ~4) | ((spot & 1) << route[2]) for route in NEAR_ROUTES]
+            parts.append(flip(block, devices, masks) if spot else block)
     return parts
 
 

time: 42.7 us -> 42.1 us (0.986); the launches traced: 42.9 us -> 41.5 us
  starting transfers between devices: 14.8 us -> 12.7 us
  Pallas kernels: 4.01 us -> 5.54 us
  blocking collectives: 12.5 us -> 11.4 us
    ppermute x7, starting transfers between devices: 14.1 us -> 12.1 us  [flip(): return lax.ppermute(value, AXES, pairs)]
    pallas_call x1, Pallas kernels: 2.76 us -> 4.3 us  [fast_ladder(): pl.pallas_call(functools.partial(ladder_kernel, block_rows, wide // 4), o...]
    all_to_all x1, blocking collectives: 12.5 us -> 11.4 us  [shards(): squares = lax.all_to_all(squares, AXES, 0, 0, tiled=True)]
  transfers between devices with their start and end apart: 9 -> 9, of which waited for: 5 -> 7; matrix products, arithmetic and copies ran while one was open for 2% -> 2% of each run, Pallas kernels for 0% -> 0%
where the time goes in v4:
time: 42.1 us; the launch traced here: 41.5 us
  starting transfers between devices  12.7 us (30%)
  blocking collectives  11.4 us (27%)
  waiting for transfers between devices  9.44 us (22%)
  Pallas kernels  5.54 us (13%)
  between operations  1.43 us (3%)
  other arithmetic  0.54 us (1%)
  local copies, waits for them, and re-layouts  0.44 us (1%)
    ppermute x7, starting transfers between devices, flip(): return lax.ppermute(value, AXES, pairs)  12.1 us
    all_to_all x1, blocking collectives, shards(): squares = lax.all_to_all(squares, AXES, 0, 0, tiled=True)  11.4 us
    ppermute x7, waiting for transfers between devices, flip(): return lax.ppermute(value, AXES, pairs)  8.16 us
    pallas_call x1, Pallas kernels, fast_ladder(): pl.pallas_call(functools.partial(ladder_kernel, block_rows, wide // 4), o...  4.3 us
    ppermute x2, waiting for transfers between devices, fast_ladder(): pieces = [s[:, 0] + lax.ppermute(s[:, 1], AXES, swap) for s in pieces]  1.29 us
  transfers between devices with their start and end apart: 9, of which 7 were waited for; matrix products, arithmetic and copies ran while one was open for 2% of the time, Pallas kernels for 0%

profile of v4, /device:TPU:0, one launch (start us, length us, event | category | flops | bytes accessed | tf_op | source)
XLA Modules:
  0.0 41.5 jit_solution(10833048176450201226)
XLA Ops:
  1.3 0.1 pad_add_fusion.place_ref
  1.4 4.3 %shard_map.86 = f32[1024,512]{1,0:T(8,128)S(1)} custom-call(s32[2]{0:T(128)S(1)} %pad_add_fusion.place_ref, s32[1]{0:T(128)S(6)} %copy.31.count_ref, bf16[6,256,1024]{2,1,0:T(8,128)(2,1)} %bitcast.53, bf16[6,256,512]{2,1,0:T(8,128)(2,1)} %bitcast.54), custom_call_target="tpu_custom_call" | custom-call | tf_op jit(solution)/shard_map/pallas_call | solution.py:99
  5.7 0.2 fusion.2
  5.8 0.0 copy-start.3
  5.9 0.1 collective-permute-start.4
  6.0 0.6 %collective-permute-start = (f32[2,4,32,512]{3,2,1,0:T(8,128)S(1)}, f32[2,4,32,512]{3,2,1,0:T(8,128)S(1)}, u32[]{:S(2)}, u32[]{:S(2)}) collective-permute-start(f32[2,4,32,512]{3,2,1,0:T(8,128)S(1)} %slice_bitcast_fusion.2), channel_id=1, source_target_pairs={{0,1},{1,0},{2,3},{3,2},{4,5},{5,4},{6,7},{7,6},{8,9},{9,8},{10,11... | collective-permute-start | bytes 1572872 | tf_op jit(solution)/shard_map/ppermute | solution.py:122
  6.6 0.0 copy-done.3
  6.6 0.0 copy-start.2
  6.6 1.3 %collective-permute-done.4 = f32[2,4,32,512]{3,2,1,0:T(8,128)S(1)} collective-permute-done((f32[2,4,32,512]{3,2,1,0:T(8,128)S(1)}, f32[2,4,32,512]{3,2,1,0:T(8,128)S(1)}, u32[]{:S(2)}, u32[]{:S(2)}) %collective-permute-start.4) | collective-permute-done | bytes 524320 | tf_op jit(solution)/shard_map/ppermute | solution.py:122
  7.9 0.1 fusion
  8.0 1.5 %collective-permute-start.5 = (f32[2,2,32,512]{3,2,1,0:T(8,128)S(1)}, f32[2,2,32,512]{3,2,1,0:T(8,128)S(1)}, u32[]{:S(2)}, u32[]{:S(2)}) collective-permute-start(f32[2,2,32,512]{3,2,1,0:T(8,128)S(1)} %slice.101), channel_id=1, source_target_pairs={{0,2},{1,5},{2,0},{3,7},{4,6},{5,1},{6,4},{7,3},{8,10},{9,13},{10,... | collective-permute-start | bytes 786440 | tf_op jit(solution)/shard_map/ppermute | solution.py:90
  9.5 0.0 collective-permute-done
  9.5 0.1 fusion.1
  9.5 0.0 copy-start
  9.6 0.0 copy-start.1
  9.6 1.6 %collective-permute-start.1 = (f32[2,2,32,512]{3,2,1,0:T(8,128)S(1)}, f32[2,2,32,512]{3,2,1,0:T(8,128)S(1)}, u32[]{:S(2)}, u32[]{:S(2)}) collective-permute-start(f32[2,2,32,512]{3,2,1,0:T(8,128)S(1)} %slice.92), channel_id=1, source_target_pairs={{0,8},{1,5},{2,10},{3,7},{4,12},{5,1},{6,14},{7,3},{8,0},{9,13},{1... | collective-permute-start | bytes 786440 | tf_op jit(solution)/shard_map/ppermute | solution.py:90
  11.2 0.0 copy-done.2
  11.2 0.2 select_reduce_fusion
  11.4 3.0 %collective-permute-done.5 = f32[2,2,32,512]{3,2,1,0:T(8,128)S(1)} collective-permute-done((f32[2,2,32,512]{3,2,1,0:T(8,128)S(1)}, f32[2,2,32,512]{3,2,1,0:T(8,128)S(1)}, u32[]{:S(2)}, u32[]{:S(2)}) %collective-permute-start.5) | collective-permute-done | bytes 262176 | tf_op jit(solution)/shard_map/ppermute | solution.py:90
  14.5 1.0 %collective-permute-start.6 = (f32[2,1,32,512]{3,2,1,0:T(8,128)S(1)}, f32[2,1,32,512]{3,2,1,0:T(8,128)S(1)}, u32[]{:S(2)}, u32[]{:S(2)}) collective-permute-start(f32[2,1,32,512]{3,2,1,0:T(8,128)S(1)} %slice.103), channel_id=1, source_target_pairs={{0,4},{1,3},{2,6},{3,1},{4,0},{5,7},{6,2},{7,5},{8,12},{9,11},{10,... | collective-permute-start | bytes 393224 | tf_op jit(solution)/shard_map/ppermute | solution.py:90
  15.5 0.6 %collective-permute-done.1 = f32[2,2,32,512]{3,2,1,0:T(8,128)S(1)} collective-permute-done((f32[2,2,32,512]{3,2,1,0:T(8,128)S(1)}, f32[2,2,32,512]{3,2,1,0:T(8,128)S(1)}, u32[]{:S(2)}, u32[]{:S(2)}) %collective-permute-start.1) | collective-permute-done | bytes 262176 | tf_op jit(solution)/shard_map/ppermute | solution.py:90
  16.1 1.8 %collective-permute-start.2 = (f32[2,1,32,512]{3,2,1,0:T(8,128)S(1)}, f32[2,1,32,512]{3,2,1,0:T(8,128)S(1)}, u32[]{:S(2)}, u32[]{:S(2)}) collective-permute-start(f32[2,1,32,512]{3,2,1,0:T(8,128)S(1)} %slice.94), channel_id=1, source_target_pairs={{0,4},{1,3},{2,6},{3,1},{4,0},{5,7},{6,2},{7,5},{8,12},{9,11},{10,... | collective-permute-start | bytes 393224 | tf_op jit(solution)/shard_map/ppermute | solution.py:90
  17.8 1.7 %collective-permute-done.6 = f32[2,1,32,512]{3,2,1,0:T(8,128)S(1)} collective-permute-done((f32[2,1,32,512]{3,2,1,0:T(8,128)S(1)}, f32[2,1,32,512]{3,2,1,0:T(8,128)S(1)}, u32[]{:S(2)}, u32[]{:S(2)}) %collective-permute-start.6) | collective-permute-done | bytes 131104 | tf_op jit(solution)/shard_map/ppermute | solution.py:90
  19.6 2.6 %collective-permute-start.7 = (f32[32,512]{1,0:T(8,128)S(1)}, f32[32,512]{1,0:T(8,128)S(1)}, u32[]{:S(2)}, u32[]{:S(2)}) collective-permute-start(f32[32,512]{1,0:T(8,128)S(1)} %get-tuple-element.11), channel_id=1, source_target_pairs={{0,16},{1,17},{2,18},{3,19},{4,20},{5,21},{6,22},{7,23},{8,24},{9,... | collective-permute-start | bytes 196616 | tf_op jit(solution)/shard_map/ppermute | solution.py:90
  22.1 2.4 %collective-permute-start.8 = (f32[32,512]{1,0:T(8,128)S(1)}, f32[32,512]{1,0:T(8,128)S(1)}, u32[]{:S(2)}, u32[]{:S(2)}) collective-permute-start(f32[32,512]{1,0:T(8,128)S(1)} %get-tuple-element.10), channel_id=1, source_target_pairs={{0,24},{1,25},{2,26},{3,27},{4,28},{5,29},{6,30},{7,31},{8,16},{9,... | collective-permute-start | bytes 196616 | tf_op jit(solution)/shard_map/ppermute | solution.py:90
  24.5 0.0 collective-permute-done.2
  24.6 1.3 %collective-permute-start.3 = (f32[32,512]{1,0:T(8,128)S(1)}, f32[32,512]{1,0:T(8,128)S(1)}, u32[]{:S(2)}, u32[]{:S(2)}) collective-permute-start(f32[32,512]{1,0:T(8,128)S(1)} %get-tuple-element.12), channel_id=1, source_target_pairs={{0,2},{1,9},{2,0},{3,11},{4,6},{5,13},{6,4},{7,15},{8,10},{9,1},{1... | collective-permute-start | bytes 196616 | tf_op jit(solution)/shard_map/ppermute | solution.py:90
  25.9 0.1 copy.25.refs_5_
  26.0 0.2 collective-permute-done.7.refs_2_
  26.1 2.1 %collective-permute-done.8.refs_3_ = f32[32,512]{1,0:T(8,128)S(1)} collective-permute-done((f32[32,512]{1,0:T(8,128)S(1)}, f32[32,512]{1,0:T(8,128)S(1)}, u32[]{:S(2)}, u32[]{:S(2)}) %collective-permute-start.8) | collective-permute-done | bytes 65568 | tf_op jit(solution)/shard_map/ppermute | solution.py:90
  28.2 0.6 %collective-permute-done.3.refs_1_ = f32[32,512]{1,0:T(8,128)S(1)} collective-permute-done((f32[32,512]{1,0:T(8,128)S(1)}, f32[32,512]{1,0:T(8,128)S(1)}, u32[]{:S(2)}, u32[]{:S(2)}) %collective-permute-start.3) | collective-permute-done | bytes 65568 | tf_op jit(solution)/shard_map/ppermute | solution.py:90
  28.9 0.0 copy-done
  28.9 0.0 copy-done.1
  28.9 0.7 %shard_map.87 = (f32[32,512]{1,0:T(8,128)}, f32[32,128]{1,0:T(8,128)S(1)}) custom-call(f32[32,512]{1,0:T(8,128)S(1)} %get-tuple-element.13.refs_0_, f32[32,512]{1,0:T(8,128)S(1)} %collective-permute-done.3.refs_1_, f32[32,512]{1,0:T(8,128)S(1)} %collective-permute-done.7.refs_2_, f32[32,512]{1,0:T(8,128)S(1)} %collective-permute-done.8.refs_3_, ...), custom_call_target="tpu_custom_call" | custom-call | tf_op jit(solution)/shard_map/pallas_call | solution.py:167
  29.6 11.4 %all_to_all.11 = f32[32,1,128]{2,1,0:T(1,128)S(1)} all-to-all(f32[32,1,128]{2,1,0:T(1,128)S(1)} %bitcast.47), channel_id=1, replica_groups=mesh['wide'=16,'narrow'=2] {'wide','narrow'}, dimensions={0} | all-to-all | bytes 32768 | tf_op jit(solution)/shard_map/all_to_all | solution.py:175
  41.0 0.5 %shard_map.88 = f32[1,1]{1,0:T(1,128)} custom-call(f32[32,128]{1,0:T(8,128)S(1)} %bitcast.46), custom_call_target="tpu_custom_call" | custom-call | tf_op jit(solution)/shard_map/pallas_call | solution.py:176
  (14 shorter events, 0.3 us)
Async XLA Ops:
  5.8 0.7 %copy-start.3 = (s32[32,2]{0,1:T(2,128)S(1)}, s32[32,2]{0,1:T(2,128)}, u32[]{:S(2)}) copy-start(s32[32,2]{0,1:T(2,128)} %param.10) | copy-start | bytes 772
  5.9 2.0 %collective-permute-start.4 = (f32[2,4,32,512]{3,2,1,0:T(8,128)S(1)}, f32[2,4,32,512]{3,2,1,0:T(8,128)S(1)}, u32[]{:S(2)}, u32[]{:S(2)}) collective-permute-start(f32[2,4,32,512]{3,2,1,0:T(8,128)S(1)} %slice_bitcast_fusion), channel_id=1, source_target_pairs={{0,1},{1,0},{2,3},{3,2},{4,5},{5,4},{6,7},{7,6},{8,9},{9,8},{10,11... | collective-permute-start | bytes 1572872 | tf_op jit(solution)/shard_map/ppermute | solution.py:122
  6.0 3.4 %collective-permute-start = (f32[2,4,32,512]{3,2,1,0:T(8,128)S(1)}, f32[2,4,32,512]{3,2,1,0:T(8,128)S(1)}, u32[]{:S(2)}, u32[]{:S(2)}) collective-permute-start(f32[2,4,32,512]{3,2,1,0:T(8,128)S(1)} %slice_bitcast_fusion.2), channel_id=1, source_target_pairs={{0,1},{1,0},{2,3},{3,2},{4,5},{5,4},{6,7},{7,6},{8,9},{9,8},{10,11... | collective-permute-start | bytes 1572872 | tf_op jit(solution)/shard_map/ppermute | solution.py:122
  6.6 4.7 %copy-start.2 = (f32[576]{0:T(1024)S(1)}, f32[576]{0:T(1024)}, u32[]{:S(2)}) copy-start(f32[576]{0:T(1024)} %param.11) | copy-start | bytes 6916
  8.0 6.4 %collective-permute-start.5 = (f32[2,2,32,512]{3,2,1,0:T(8,128)S(1)}, f32[2,2,32,512]{3,2,1,0:T(8,128)S(1)}, u32[]{:S(2)}, u32[]{:S(2)}) collective-permute-start(f32[2,2,32,512]{3,2,1,0:T(8,128)S(1)} %slice.101), channel_id=1, source_target_pairs={{0,2},{1,5},{2,0},{3,7},{4,6},{5,1},{6,4},{7,3},{8,10},{9,13},{10,... | collective-permute-start | bytes 786440 | tf_op jit(solution)/shard_map/ppermute | solution.py:90
  9.5 19.3 %copy-start = (f32[32,512]{1,0:T(8,128)S(1)}, f32[32,512]{1,0:T(8,128)}, u32[]{:S(2)}) copy-start(f32[32,512]{1,0:T(8,128)} %refs_4_.1) | copy-start | bytes 196612
  9.6 19.3 %copy-start.1 = (f32[512]{0:T(512)S(1)}, f32[512]{0:T(512)}, u32[]{:S(2)}) copy-start(f32[512]{0:T(512)} %param.12) | copy-start | bytes 6148
  9.6 6.4 %collective-permute-start.1 = (f32[2,2,32,512]{3,2,1,0:T(8,128)S(1)}, f32[2,2,32,512]{3,2,1,0:T(8,128)S(1)}, u32[]{:S(2)}, u32[]{:S(2)}) collective-permute-start(f32[2,2,32,512]{3,2,1,0:T(8,128)S(1)} %slice.92), channel_id=1, source_target_pairs={{0,8},{1,5},{2,10},{3,7},{4,12},{5,1},{6,14},{7,3},{8,0},{9,13},{1... | collective-permute-start | bytes 786440 | tf_op jit(solution)/shard_map/ppermute | solution.py:90
  14.5 5.0 %collective-permute-start.6 = (f32[2,1,32,512]{3,2,1,0:T(8,128)S(1)}, f32[2,1,32,512]{3,2,1,0:T(8,128)S(1)}, u32[]{:S(2)}, u32[]{:S(2)}) collective-permute-start(f32[2,1,32,512]{3,2,1,0:T(8,128)S(1)} %slice.103), channel_id=1, source_target_pairs={{0,4},{1,3},{2,6},{3,1},{4,0},{5,7},{6,2},{7,5},{8,12},{9,11},{10,... | collective-permute-start | bytes 393224 | tf_op jit(solution)/shard_map/ppermute | solution.py:90
  16.1 8.4 %collective-permute-start.2 = (f32[2,1,32,512]{3,2,1,0:T(8,128)S(1)}, f32[2,1,32,512]{3,2,1,0:T(8,128)S(1)}, u32[]{:S(2)}, u32[]{:S(2)}) collective-permute-start(f32[2,1,32,512]{3,2,1,0:T(8,128)S(1)} %slice.94), channel_id=1, source_target_pairs={{0,4},{1,3},{2,6},{3,1},{4,0},{5,7},{6,2},{7,5},{8,12},{9,11},{10,... | collective-permute-start | bytes 393224 | tf_op jit(solution)/shard_map/ppermute | solution.py:90
  19.6 6.6 %collective-permute-start.7 = (f32[32,512]{1,0:T(8,128)S(1)}, f32[32,512]{1,0:T(8,128)S(1)}, u32[]{:S(2)}, u32[]{:S(2)}) collective-permute-start(f32[32,512]{1,0:T(8,128)S(1)} %get-tuple-element.11), channel_id=1, source_target_pairs={{0,16},{1,17},{2,18},{3,19},{4,20},{5,21},{6,22},{7,23},{8,24},{9,... | collective-permute-start | bytes 196616 | tf_op jit(solution)/shard_map/ppermute | solution.py:90
  22.1 6.1 %collective-permute-start.8 = (f32[32,512]{1,0:T(8,128)S(1)}, f32[32,512]{1,0:T(8,128)S(1)}, u32[]{:S(2)}, u32[]{:S(2)}) collective-permute-start(f32[32,512]{1,0:T(8,128)S(1)} %get-tuple-element.10), channel_id=1, source_target_pairs={{0,24},{1,25},{2,26},{3,27},{4,28},{5,29},{6,30},{7,31},{8,16},{9,... | collective-permute-start | bytes 196616 | tf_op jit(solution)/shard_map/ppermute | solution.py:90
  24.6 4.3 %collective-permute-start.3 = (f32[32,512]{1,0:T(8,128)S(1)}, f32[32,512]{1,0:T(8,128)S(1)}, u32[]{:S(2)}, u32[]{:S(2)}) collective-permute-start(f32[32,512]{1,0:T(8,128)S(1)} %get-tuple-element.12), channel_id=1, source_target_pairs={{0,2},{1,9},{2,0},{3,11},{4,6},{5,13},{6,4},{7,15},{8,10},{9,1},{1... | collective-permute-start | bytes 196616 | tf_op jit(solution)/shard_map/ppermute | solution.py:90

commit v5 on v4

--- a/solution.py
+++ b/solution.py
@@ -80,7 +80,8 @@
     square_ref[...] = jnp.full(square_ref.shape, jnp.sum(update * update))
 
 
-def norm_kernel(entries, squares_ref, norm_ref):
+def norm_kernel(entries, squares_ref, update_ref, norm_ref, out_ref):
+    out_ref[...] = update_ref[...]
     total = jnp.sum(squares_ref[...], axis=0, keepdims=True)
     norm_ref[...] = jnp.sqrt(total / entries)[:, :1]
 
@@ -167,17 +168,21 @@
         update, squares = pl.pallas_call(
             functools.partial(update_kernel, len(parts)),
             out_shape=[
-                jax.ShapeDtypeStruct(other_terms.shape, jnp.float32),
+                pltpu.VMEM(other_terms.shape, jnp.float32),
                 pltpu.VMEM((devices, 128), jnp.float32),
             ],
             compiler_params=pltpu.CompilerParams(vmem_limit_bytes=4 << 20),
         )(*parts, other_terms, virtual_sum, occupied)
         squares = lax.all_to_all(squares, AXES, 0, 0, tiled=True)
-        update_norm = pl.pallas_call(
+        update_norm, update = pl.pallas_call(
             functools.partial(norm_kernel, rows * width),
-            out_shape=jax.ShapeDtypeStruct((1, 1), jnp.float32),
+            out_shape=[
+                jax.ShapeDtypeStruct((1, 1), jnp.float32),
+                jax.ShapeDtypeStruct(other_terms.shape, jnp.float32),
+            ],
             compiler_params=pltpu.CompilerParams(vmem_limit_bytes=4 << 20),
-        )(squares).reshape(())
+        )(squares, update)
+        update_norm = update_norm.reshape(())
     else:
         ladder = plain_ladder(tile_block, amp_rows, tile_count)
         update = (ladder + other_terms) / (occupied - virtual_sum)

time: 42.1 us -> 41.6 us (0.988)
  starting transfers between devices: 12.7 us -> 15.7 us
  Pallas kernels: 5.54 us -> 3.11 us
  waiting for transfers between devices: 9.44 us -> 8.82 us
  blocking collectives: 11.4 us -> 10.9 us
    ppermute x7, starting transfers between devices: 12.1 us -> 14.6 us  [flip(): return lax.ppermute(value, AXES, pairs)]
    pallas_call x1, Pallas kernels: 4.3 us -> 2.26 us  [fast_ladder(): pl.pallas_call(functools.partial(ladder_kernel, block_rows, wide // 4), o...]
    ppermute x7, waiting for transfers between devices: 8.16 us -> 7.43 us  [flip(): return lax.ppermute(value, AXES, pairs)]
    all_to_all x1, blocking collectives: 11.4 us -> 10.9 us  [shards(): squares = lax.all_to_all(squares, AXES, 0, 0, tiled=True)]
    ppermute x2, starting transfers between devices: 0.63 us -> 1.1 us  [fast_ladder(): pieces = [s[:, 0] + lax.ppermute(s[:, 1], AXES, swap) for s in pieces]]
  transfers between devices with their start and end apart: 9 -> 9, of which waited for: 7 -> 4; matrix products, arithmetic and copies ran while one was open for 2% -> 2% of each run, Pallas kernels for 0% -> 0%
where the time goes in v5:
time: 41.6 us; the launch traced here: 41 us
  starting transfers between devices  15.7 us (38%)
  blocking collectives  10.9 us (26%)
  waiting for transfers between devices  8.82 us (21%)
  Pallas kernels  3.11 us (7%)
  between operations  1.44 us (3%)
  other arithmetic  0.54 us (1%)
  local copies, waits for them, and re-layouts  0.44 us (1%)
    ppermute x7, starting transfers between devices, flip(): return lax.ppermute(value, AXES, pairs)  14.6 us
    all_to_all x1, blocking collectives, shards(): squares = lax.all_to_all(squares, AXES, 0, 0, tiled=True)  10.9 us
    ppermute x7, waiting for transfers between devices, flip(): return lax.ppermute(value, AXES, pairs)  7.43 us
    pallas_call x1, Pallas kernels, fast_ladder(): pl.pallas_call(functools.partial(ladder_kernel, block_rows, wide // 4), o...  2.26 us
    ppermute x2, waiting for transfers between devices, fast_ladder(): pieces = [s[:, 0] + lax.ppermute(s[:, 1], AXES, swap) for s in pieces]  1.39 us
    ppermute x2, starting transfers between devices, fast_ladder(): pieces = [s[:, 0] + lax.ppermute(s[:, 1], AXES, swap) for s in pieces]  1.1 us
  transfers between devices with their start and end apart: 9, of which 4 were waited for; matrix products, arithmetic and copies ran while one was open for 2% of the time, Pallas kernels for 0%

profile of v5, /device:TPU:0, one launch (start us, length us, event | category | flops | bytes accessed | tf_op | source)
XLA Modules:
  0.0 41.0 jit_solution(17126347775933027539)
XLA Ops:
  1.3 0.1 pad_add_fusion.place_ref
  1.4 2.3 %shard_map.86 = f32[1024,512]{1,0:T(8,128)S(1)} custom-call(s32[2]{0:T(128)S(1)} %pad_add_fusion.place_ref, s32[1]{0:T(128)S(6)} %copy.31.count_ref, bf16[6,256,1024]{2,1,0:T(8,128)(2,1)} %bitcast.53, bf16[6,256,512]{2,1,0:T(8,128)(2,1)} %bitcast.54), custom_call_target="tpu_custom_call" | custom-call | tf_op jit(solution)/shard_map/pallas_call | solution.py:100
  3.6 0.2 fusion.2
  3.8 0.0 copy-start.3
  3.9 1.0 %collective-permute-start.4 = (f32[2,4,32,512]{3,2,1,0:T(8,128)S(1)}, f32[2,4,32,512]{3,2,1,0:T(8,128)S(1)}, u32[]{:S(2)}, u32[]{:S(2)}) collective-permute-start(f32[2,4,32,512]{3,2,1,0:T(8,128)S(1)} %slice_bitcast_fusion), channel_id=1, source_target_pairs={{0,1},{1,0},{2,3},{3,2},{4,5},{5,4},{6,7},{7,6},{8,9},{9,8},{10,11... | collective-permute-start | bytes 1572872 | tf_op jit(solution)/shard_map/ppermute | solution.py:123
  4.9 0.1 collective-permute-start
  5.0 0.0 copy-done.3
  5.0 0.0 copy-start.2
  5.0 1.4 %collective-permute-done.4 = f32[2,4,32,512]{3,2,1,0:T(8,128)S(1)} collective-permute-done((f32[2,4,32,512]{3,2,1,0:T(8,128)S(1)}, f32[2,4,32,512]{3,2,1,0:T(8,128)S(1)}, u32[]{:S(2)}, u32[]{:S(2)}) %collective-permute-start.4) | collective-permute-done | bytes 524320 | tf_op jit(solution)/shard_map/ppermute | solution.py:123
  6.4 0.1 fusion
  6.5 3.9 %collective-permute-start.5 = (f32[2,2,32,512]{3,2,1,0:T(8,128)S(1)}, f32[2,2,32,512]{3,2,1,0:T(8,128)S(1)}, u32[]{:S(2)}, u32[]{:S(2)}) collective-permute-start(f32[2,2,32,512]{3,2,1,0:T(8,128)S(1)} %slice.101), channel_id=1, source_target_pairs={{0,2},{1,5},{2,0},{3,7},{4,6},{5,1},{6,4},{7,3},{8,10},{9,13},{10,... | collective-permute-start | bytes 786440 | tf_op jit(solution)/shard_map/ppermute | solution.py:91
  10.5 0.0 collective-permute-done
  10.5 0.1 fusion.1
  10.5 0.0 copy-start
  10.6 0.0 copy-start.1
  10.6 0.1 collective-permute-start.1
  10.7 0.0 copy-done.2
  10.7 0.2 select_reduce_fusion
  10.9 3.9 %collective-permute-done.5 = f32[2,2,32,512]{3,2,1,0:T(8,128)S(1)} collective-permute-done((f32[2,2,32,512]{3,2,1,0:T(8,128)S(1)}, f32[2,2,32,512]{3,2,1,0:T(8,128)S(1)}, u32[]{:S(2)}, u32[]{:S(2)}) %collective-permute-start.5) | collective-permute-done | bytes 262176 | tf_op jit(solution)/shard_map/ppermute | solution.py:91
  14.9 2.1 %collective-permute-start.6 = (f32[2,1,32,512]{3,2,1,0:T(8,128)S(1)}, f32[2,1,32,512]{3,2,1,0:T(8,128)S(1)}, u32[]{:S(2)}, u32[]{:S(2)}) collective-permute-start(f32[2,1,32,512]{3,2,1,0:T(8,128)S(1)} %slice.103), channel_id=1, source_target_pairs={{0,4},{1,3},{2,6},{3,1},{4,0},{5,7},{6,2},{7,5},{8,12},{9,11},{10,... | collective-permute-start | bytes 393224 | tf_op jit(solution)/shard_map/ppermute | solution.py:91
  17.0 0.0 collective-permute-done.1
  17.1 2.1 %collective-permute-start.2 = (f32[2,1,32,512]{3,2,1,0:T(8,128)S(1)}, f32[2,1,32,512]{3,2,1,0:T(8,128)S(1)}, u32[]{:S(2)}, u32[]{:S(2)}) collective-permute-start(f32[2,1,32,512]{3,2,1,0:T(8,128)S(1)} %slice.94), channel_id=1, source_target_pairs={{0,4},{1,3},{2,6},{3,1},{4,0},{5,7},{6,2},{7,5},{8,12},{9,11},{10,... | collective-permute-start | bytes 393224 | tf_op jit(solution)/shard_map/ppermute | solution.py:91
  19.2 0.7 %collective-permute-done.6 = f32[2,1,32,512]{3,2,1,0:T(8,128)S(1)} collective-permute-done((f32[2,1,32,512]{3,2,1,0:T(8,128)S(1)}, f32[2,1,32,512]{3,2,1,0:T(8,128)S(1)}, u32[]{:S(2)}, u32[]{:S(2)}) %collective-permute-start.6) | collective-permute-done | bytes 131104 | tf_op jit(solution)/shard_map/ppermute | solution.py:91
  20.0 3.2 %collective-permute-start.7 = (f32[32,512]{1,0:T(8,128)S(1)}, f32[32,512]{1,0:T(8,128)S(1)}, u32[]{:S(2)}, u32[]{:S(2)}) collective-permute-start(f32[32,512]{1,0:T(8,128)S(1)} %get-tuple-element.15), channel_id=1, source_target_pairs={{0,16},{1,17},{2,18},{3,19},{4,20},{5,21},{6,22},{7,23},{8,24},{9,... | collective-permute-start | bytes 196616 | tf_op jit(solution)/shard_map/ppermute | solution.py:91
  23.2 1.1 %collective-permute-start.8 = (f32[32,512]{1,0:T(8,128)S(1)}, f32[32,512]{1,0:T(8,128)S(1)}, u32[]{:S(2)}, u32[]{:S(2)}) collective-permute-start(f32[32,512]{1,0:T(8,128)S(1)} %get-tuple-element.14), channel_id=1, source_target_pairs={{0,24},{1,25},{2,26},{3,27},{4,28},{5,29},{6,30},{7,31},{8,16},{9,... | collective-permute-start | bytes 196616 | tf_op jit(solution)/shard_map/ppermute | solution.py:91
  24.2 0.0 collective-permute-done.2
  24.3 2.1 %collective-permute-start.3 = (f32[32,512]{1,0:T(8,128)S(1)}, f32[32,512]{1,0:T(8,128)S(1)}, u32[]{:S(2)}, u32[]{:S(2)}) collective-permute-start(f32[32,512]{1,0:T(8,128)S(1)} %get-tuple-element.16), channel_id=1, source_target_pairs={{0,2},{1,9},{2,0},{3,11},{4,6},{5,13},{6,4},{7,15},{8,10},{9,1},{1... | collective-permute-start | bytes 196616 | tf_op jit(solution)/shard_map/ppermute | solution.py:91
  26.4 0.1 copy.25.refs_5_
  26.4 0.0 collective-permute-done.7.refs_2_
  26.4 2.8 %collective-permute-done.8.refs_3_ = f32[32,512]{1,0:T(8,128)S(1)} collective-permute-done((f32[32,512]{1,0:T(8,128)S(1)}, f32[32,512]{1,0:T(8,128)S(1)}, u32[]{:S(2)}, u32[]{:S(2)}) %collective-permute-start.8) | collective-permute-done | bytes 65568 | tf_op jit(solution)/shard_map/ppermute | solution.py:91
  29.2 0.0 collective-permute-done.3.refs_1_
  29.2 0.0 copy-done
  29.2 0.0 copy-done.1
  29.2 0.2 shard_map.87
  29.5 10.9 %all_to_all.11 = f32[32,1,128]{2,1,0:T(1,128)S(1)} all-to-all(f32[32,1,128]{2,1,0:T(1,128)S(1)} %bitcast.47), channel_id=1, replica_groups=mesh['wide'=16,'narrow'=2] {'wide','narrow'}, dimensions={0} | all-to-all | bytes 32768 | tf_op jit(solution)/shard_map/all_to_all | solution.py:176
  40.4 0.6 %shard_map.88 = (f32[1,1]{1,0:T(1,128)}, f32[32,512]{1,0:T(8,128)}) custom-call(f32[32,128]{1,0:T(8,128)S(1)} %bitcast.46, f32[32,512]{1,0:T(8,128)S(1)} %get-tuple-element.7.update_ref), custom_call_target="tpu_custom_call" | custom-call | tf_op jit(solution)/shard_map/pallas_call | solution.py:177
  (14 shorter events, 0.3 us)
Async XLA Ops:
  3.8 1.2 %copy-start.3 = (s32[32,2]{0,1:T(2,128)S(1)}, s32[32,2]{0,1:T(2,128)}, u32[]{:S(2)}) copy-start(s32[32,2]{0,1:T(2,128)} %param.10) | copy-start | bytes 772
  3.9 2.6 %collective-permute-start.4 = (f32[2,4,32,512]{3,2,1,0:T(8,128)S(1)}, f32[2,4,32,512]{3,2,1,0:T(8,128)S(1)}, u32[]{:S(2)}, u32[]{:S(2)}) collective-permute-start(f32[2,4,32,512]{3,2,1,0:T(8,128)S(1)} %slice_bitcast_fusion), channel_id=1, source_target_pairs={{0,1},{1,0},{2,3},{3,2},{4,5},{5,4},{6,7},{7,6},{8,9},{9,8},{10,11... | collective-permute-start | bytes 1572872 | tf_op jit(solution)/shard_map/ppermute | solution.py:123
  4.9 5.5 %collective-permute-start = (f32[2,4,32,512]{3,2,1,0:T(8,128)S(1)}, f32[2,4,32,512]{3,2,1,0:T(8,128)S(1)}, u32[]{:S(2)}, u32[]{:S(2)}) collective-permute-start(f32[2,4,32,512]{3,2,1,0:T(8,128)S(1)} %slice_bitcast_fusion.2), channel_id=1, source_target_pairs={{0,1},{1,0},{2,3},{3,2},{4,5},{5,4},{6,7},{7,6},{8,9},{9,8},{10,11... | collective-permute-start | bytes 1572872 | tf_op jit(solution)/shard_map/ppermute | solution.py:123
  5.0 5.7 %copy-start.2 = (f32[576]{0:T(1024)S(1)}, f32[576]{0:T(1024)}, u32[]{:S(2)}) copy-start(f32[576]{0:T(1024)} %param.11) | copy-start | bytes 6916
  6.5 8.3 %collective-permute-start.5 = (f32[2,2,32,512]{3,2,1,0:T(8,128)S(1)}, f32[2,2,32,512]{3,2,1,0:T(8,128)S(1)}, u32[]{:S(2)}, u32[]{:S(2)}) collective-permute-start(f32[2,2,32,512]{3,2,1,0:T(8,128)S(1)} %slice.101), channel_id=1, source_target_pairs={{0,2},{1,5},{2,0},{3,7},{4,6},{5,1},{6,4},{7,3},{8,10},{9,13},{10,... | collective-permute-start | bytes 786440 | tf_op jit(solution)/shard_map/ppermute | solution.py:91
  10.5 18.7 %copy-start = (f32[32,512]{1,0:T(8,128)S(1)}, f32[32,512]{1,0:T(8,128)}, u32[]{:S(2)}) copy-start(f32[32,512]{1,0:T(8,128)} %refs_4_.1) | copy-start | bytes 196612
  10.6 18.7 %copy-start.1 = (f32[512]{0:T(512)S(1)}, f32[512]{0:T(512)}, u32[]{:S(2)}) copy-start(f32[512]{0:T(512)} %param.12) | copy-start | bytes 6148
  10.6 6.4 %collective-permute-start.1 = (f32[2,2,32,512]{3,2,1,0:T(8,128)S(1)}, f32[2,2,32,512]{3,2,1,0:T(8,128)S(1)}, u32[]{:S(2)}, u32[]{:S(2)}) collective-permute-start(f32[2,2,32,512]{3,2,1,0:T(8,128)S(1)} %slice.92), channel_id=1, source_target_pairs={{0,8},{1,5},{2,10},{3,7},{4,12},{5,1},{6,14},{7,3},{8,0},{9,13},{1... | collective-permute-start | bytes 786440 | tf_op jit(solution)/shard_map/ppermute | solution.py:91
  14.9 5.1 %collective-permute-start.6 = (f32[2,1,32,512]{3,2,1,0:T(8,128)S(1)}, f32[2,1,32,512]{3,2,1,0:T(8,128)S(1)}, u32[]{:S(2)}, u32[]{:S(2)}) collective-permute-start(f32[2,1,32,512]{3,2,1,0:T(8,128)S(1)} %slice.103), channel_id=1, source_target_pairs={{0,4},{1,3},{2,6},{3,1},{4,0},{5,7},{6,2},{7,5},{8,12},{9,11},{10,... | collective-permute-start | bytes 393224 | tf_op jit(solution)/shard_map/ppermute | solution.py:91
  17.1 7.1 %collective-permute-start.2 = (f32[2,1,32,512]{3,2,1,0:T(8,128)S(1)}, f32[2,1,32,512]{3,2,1,0:T(8,128)S(1)}, u32[]{:S(2)}, u32[]{:S(2)}) collective-permute-start(f32[2,1,32,512]{3,2,1,0:T(8,128)S(1)} %slice.94), channel_id=1, source_target_pairs={{0,4},{1,3},{2,6},{3,1},{4,0},{5,7},{6,2},{7,5},{8,12},{9,11},{10,... | collective-permute-start | bytes 393224 | tf_op jit(solution)/shard_map/ppermute | solution.py:91
  20.0 6.5 %collective-permute-start.7 = (f32[32,512]{1,0:T(8,128)S(1)}, f32[32,512]{1,0:T(8,128)S(1)}, u32[]{:S(2)}, u32[]{:S(2)}) collective-permute-start(f32[32,512]{1,0:T(8,128)S(1)} %get-tuple-element.15), channel_id=1, source_target_pairs={{0,16},{1,17},{2,18},{3,19},{4,20},{5,21},{6,22},{7,23},{8,24},{9,... | collective-permute-start | bytes 196616 | tf_op jit(solution)/shard_map/ppermute | solution.py:91
  23.2 6.1 %collective-permute-start.8 = (f32[32,512]{1,0:T(8,128)S(1)}, f32[32,512]{1,0:T(8,128)S(1)}, u32[]{:S(2)}, u32[]{:S(2)}) collective-permute-start(f32[32,512]{1,0:T(8,128)S(1)} %get-tuple-element.14), channel_id=1, source_target_pairs={{0,24},{1,25},{2,26},{3,27},{4,28},{5,29},{6,30},{7,31},{8,16},{9,... | collective-permute-start | bytes 196616 | tf_op jit(solution)/shard_map/ppermute | solution.py:91
  24.3 5.0 %collective-permute-start.3 = (f32[32,512]{1,0:T(8,128)S(1)}, f32[32,512]{1,0:T(8,128)S(1)}, u32[]{:S(2)}, u32[]{:S(2)}) collective-permute-start(f32[32,512]{1,0:T(8,128)S(1)} %get-tuple-element.16), channel_id=1, source_target_pairs={{0,2},{1,9},{2,0},{3,11},{4,6},{5,13},{6,4},{7,15},{8,10},{9,1},{1... | collective-permute-start | bytes 196616 | tf_op jit(solution)/shard_map/ppermute | solution.py:91

commit v6 on v5

--- a/solution.py
+++ b/solution.py
@@ -19,10 +19,10 @@
     return spot
 
 
-def ladder_kernel(block_rows, planes, place_ref, count_ref, tiles_ref, amps_ref, out_ref, tile_buf, amp_buf, tile_sem, amp_sem):
+def ladder_kernel(block_rows, planes, count_ref, tiles_ref, amps_ref, out_ref, tile_buf, amp_buf, tile_sem, amp_sem):
     slots, _, rows = tile_buf.shape
     live = count_ref[0]
-    wide_me, narrow_me = place_ref[0], place_ref[1]
+    wide_me, narrow_me = lax.axis_index("wide"), lax.axis_index("narrow")
 
     def copies(slot):
         return (
@@ -96,11 +96,10 @@
     width = amp_rows.shape[2]
     devices = wide * narrow
     block_rows = rows // devices
-    place = jnp.stack([lax.axis_index("wide"), lax.axis_index("narrow")]).astype(jnp.int32)
     partial = pl.pallas_call(
         functools.partial(ladder_kernel, block_rows, wide // 4),
         out_shape=pltpu.VMEM((rows, width), jnp.float32),
-        in_specs=[pl.BlockSpec(memory_space=pltpu.SMEM)] * 2 + [pl.BlockSpec(memory_space=pltpu.HBM)] * 2,
+        in_specs=[pl.BlockSpec(memory_space=pltpu.SMEM)] + [pl.BlockSpec(memory_space=pltpu.HBM)] * 2,
         out_specs=pl.BlockSpec(memory_space=pltpu.VMEM),
         scratch_shapes=[
             pltpu.VMEM((slots, depth, rows), tile_block.dtype),
@@ -110,7 +109,6 @@
         ],
         compiler_params=pltpu.CompilerParams(vmem_limit_bytes=32 << 20),
     )(
-        place,
         tile_count,
         pltpu.with_memory_space_constraint(tile_block, pltpu.HBM),
         pltpu.with_memory_space_constraint(amp_rows, pltpu.HBM),

time: 41.6 us -> 40.3 us (0.969); the launches traced: 41 us -> 40.8 us
  starting transfers between devices: 15.7 us -> 14.5 us
  blocking collectives: 10.9 us -> 11.8 us
  waiting for transfers between devices: 8.82 us -> 9.62 us
  Pallas kernels: 3.11 us -> 2.57 us
    ppermute x7, starting transfers between devices: 14.6 us -> 11.8 us  [flip(): return lax.ppermute(value, AXES, pairs)]
    ppermute x2, starting transfers between devices: 1.1 us -> 2.63 us  [fast_ladder(): pieces = [s[:, 0] + lax.ppermute(s[:, 1], AXES, swap) for s in pieces]]
    all_to_all x1, blocking collectives: 10.9 us -> 11.8 us  [shards(): squares = lax.all_to_all(squares, AXES, 0, 0, tiled=True)]
    ppermute x7, waiting for transfers between devices: 7.43 us -> 8.23 us  [flip(): return lax.ppermute(value, AXES, pairs)]
    pallas_call x1, Pallas kernels: 2.26 us -> 1.72 us  [fast_ladder(): pl.pallas_call(functools.partial(ladder_kernel, block_rows, wide // 4), o...]
  transfers between devices with their start and end apart: 9 -> 9, of which waited for: 4 -> 5; matrix products, arithmetic and copies ran while one was open for 2% -> 2% of each run, Pallas kernels for 0% -> 0%
where the time goes in v6:
time: 40.3 us; the launch traced here: 40.8 us
  starting transfers between devices  14.5 us (36%)
  blocking collectives  11.8 us (29%)
  waiting for transfers between devices  9.62 us (24%)
  Pallas kernels  2.57 us (6%)
  between operations  1.43 us (4%)
  other arithmetic  0.47 us (1%)
  local copies, waits for them, and re-layouts  0.44 us (1%)
    ppermute x7, starting transfers between devices, flip(): return lax.ppermute(value, AXES, pairs)  11.8 us
    all_to_all x1, blocking collectives, shards(): squares = lax.all_to_all(squares, AXES, 0, 0, tiled=True)  11.8 us
    ppermute x7, waiting for transfers between devices, flip(): return lax.ppermute(value, AXES, pairs)  8.23 us
    ppermute x2, starting transfers between devices, fast_ladder(): pieces = [s[:, 0] + lax.ppermute(s[:, 1], AXES, swap) for s in pieces]  2.63 us
    pallas_call x1, Pallas kernels, fast_ladder(): pl.pallas_call(functools.partial(ladder_kernel, block_rows, wide // 4), o...  1.72 us
    ppermute x2, waiting for transfers between devices, fast_ladder(): pieces = [s[:, 0] + lax.ppermute(s[:, 1], AXES, swap) for s in pieces]  1.39 us
  transfers between devices with their start and end apart: 9, of which 5 were waited for; matrix products, arithmetic and copies ran while one was open for 2% of the time, Pallas kernels for 0%

profile of v6, /device:TPU:0, one launch (start us, length us, event | category | flops | bytes accessed | tf_op | source)
XLA Modules:
  0.0 40.8 jit_solution(10530430358623036264)
XLA Ops:
  1.3 1.7 %shard_map.86 = f32[1024,512]{1,0:T(8,128)S(1)} custom-call(s32[1]{0:T(128)S(6)} %copy.31.count_ref, bf16[6,256,1024]{2,1,0:T(8,128)(2,1)} %bitcast.51, bf16[6,256,512]{2,1,0:T(8,128)(2,1)} %bitcast.52), custom_call_target="tpu_custom_call" | custom-call | tf_op jit(solution)/shard_map/pallas_call | solution.py:99
  3.0 0.2 fusion.2
  3.2 0.0 copy-start.3
  3.2 2.5 %collective-permute-start.4 = (f32[2,4,32,512]{3,2,1,0:T(8,128)S(1)}, f32[2,4,32,512]{3,2,1,0:T(8,128)S(1)}, u32[]{:S(2)}, u32[]{:S(2)}) collective-permute-start(f32[2,4,32,512]{3,2,1,0:T(8,128)S(1)} %slice_bitcast_fusion), channel_id=1, source_target_pairs={{0,1},{1,0},{2,3},{3,2},{4,5},{5,4},{6,7},{7,6},{8,9},{9,8},{10,11... | collective-permute-start | bytes 1572872 | tf_op jit(solution)/shard_map/ppermute | solution.py:121
  5.8 0.1 collective-permute-start
  5.9 0.0 copy-done.3
  5.9 0.0 copy-start.2
  5.9 1.4 %collective-permute-done.4 = f32[2,4,32,512]{3,2,1,0:T(8,128)S(1)} collective-permute-done((f32[2,4,32,512]{3,2,1,0:T(8,128)S(1)}, f32[2,4,32,512]{3,2,1,0:T(8,128)S(1)}, u32[]{:S(2)}, u32[]{:S(2)}) %collective-permute-start.4) | collective-permute-done | bytes 524320 | tf_op jit(solution)/shard_map/ppermute | solution.py:121
  7.3 0.1 fusion
  7.4 1.4 %collective-permute-start.5 = (f32[2,2,32,512]{3,2,1,0:T(8,128)S(1)}, f32[2,2,32,512]{3,2,1,0:T(8,128)S(1)}, u32[]{:S(2)}, u32[]{:S(2)}) collective-permute-start(f32[2,2,32,512]{3,2,1,0:T(8,128)S(1)} %slice.101), channel_id=1, source_target_pairs={{0,2},{1,5},{2,0},{3,7},{4,6},{5,1},{6,4},{7,3},{8,10},{9,13},{10,... | collective-permute-start | bytes 786440 | tf_op jit(solution)/shard_map/ppermute | solution.py:91
  8.8 0.0 collective-permute-done
  8.8 0.1 fusion.1
  8.9 0.0 copy-start
  8.9 0.0 copy-start.1
  9.0 1.6 %collective-permute-start.1 = (f32[2,2,32,512]{3,2,1,0:T(8,128)S(1)}, f32[2,2,32,512]{3,2,1,0:T(8,128)S(1)}, u32[]{:S(2)}, u32[]{:S(2)}) collective-permute-start(f32[2,2,32,512]{3,2,1,0:T(8,128)S(1)} %slice.92), channel_id=1, source_target_pairs={{0,8},{1,5},{2,10},{3,7},{4,12},{5,1},{6,14},{7,3},{8,0},{9,13},{1... | collective-permute-start | bytes 786440 | tf_op jit(solution)/shard_map/ppermute | solution.py:91
  10.6 0.0 copy-done.2
  10.6 0.2 select_reduce_fusion
  10.8 3.1 %collective-permute-done.5 = f32[2,2,32,512]{3,2,1,0:T(8,128)S(1)} collective-permute-done((f32[2,2,32,512]{3,2,1,0:T(8,128)S(1)}, f32[2,2,32,512]{3,2,1,0:T(8,128)S(1)}, u32[]{:S(2)}, u32[]{:S(2)}) %collective-permute-start.5) | collective-permute-done | bytes 262176 | tf_op jit(solution)/shard_map/ppermute | solution.py:91
  13.9 0.9 %collective-permute-start.6 = (f32[2,1,32,512]{3,2,1,0:T(8,128)S(1)}, f32[2,1,32,512]{3,2,1,0:T(8,128)S(1)}, u32[]{:S(2)}, u32[]{:S(2)}) collective-permute-start(f32[2,1,32,512]{3,2,1,0:T(8,128)S(1)} %slice.103), channel_id=1, source_target_pairs={{0,4},{1,3},{2,6},{3,1},{4,0},{5,7},{6,2},{7,5},{8,12},{9,11},{10,... | collective-permute-start | bytes 393224 | tf_op jit(solution)/shard_map/ppermute | solution.py:91
  14.9 0.6 %collective-permute-done.1 = f32[2,2,32,512]{3,2,1,0:T(8,128)S(1)} collective-permute-done((f32[2,2,32,512]{3,2,1,0:T(8,128)S(1)}, f32[2,2,32,512]{3,2,1,0:T(8,128)S(1)}, u32[]{:S(2)}, u32[]{:S(2)}) %collective-permute-start.1) | collective-permute-done | bytes 262176 | tf_op jit(solution)/shard_map/ppermute | solution.py:91
  15.5 1.2 %collective-permute-start.2 = (f32[2,1,32,512]{3,2,1,0:T(8,128)S(1)}, f32[2,1,32,512]{3,2,1,0:T(8,128)S(1)}, u32[]{:S(2)}, u32[]{:S(2)}) collective-permute-start(f32[2,1,32,512]{3,2,1,0:T(8,128)S(1)} %slice.94), channel_id=1, source_target_pairs={{0,4},{1,3},{2,6},{3,1},{4,0},{5,7},{6,2},{7,5},{8,12},{9,11},{10,... | collective-permute-start | bytes 393224 | tf_op jit(solution)/shard_map/ppermute | solution.py:91
  16.7 2.3 %collective-permute-done.6 = f32[2,1,32,512]{3,2,1,0:T(8,128)S(1)} collective-permute-done((f32[2,1,32,512]{3,2,1,0:T(8,128)S(1)}, f32[2,1,32,512]{3,2,1,0:T(8,128)S(1)}, u32[]{:S(2)}, u32[]{:S(2)}) %collective-permute-start.6) | collective-permute-done | bytes 131104 | tf_op jit(solution)/shard_map/ppermute | solution.py:91
  19.0 2.9 %collective-permute-start.7 = (f32[32,512]{1,0:T(8,128)S(1)}, f32[32,512]{1,0:T(8,128)S(1)}, u32[]{:S(2)}, u32[]{:S(2)}) collective-permute-start(f32[32,512]{1,0:T(8,128)S(1)} %get-tuple-element.15), channel_id=1, source_target_pairs={{0,16},{1,17},{2,18},{3,19},{4,20},{5,21},{6,22},{7,23},{8,24},{9,... | collective-permute-start | bytes 196616 | tf_op jit(solution)/shard_map/ppermute | solution.py:91
  22.0 1.7 %collective-permute-start.8 = (f32[32,512]{1,0:T(8,128)S(1)}, f32[32,512]{1,0:T(8,128)S(1)}, u32[]{:S(2)}, u32[]{:S(2)}) collective-permute-start(f32[32,512]{1,0:T(8,128)S(1)} %get-tuple-element.14), channel_id=1, source_target_pairs={{0,24},{1,25},{2,26},{3,27},{4,28},{5,29},{6,30},{7,31},{8,16},{9,... | collective-permute-start | bytes 196616 | tf_op jit(solution)/shard_map/ppermute | solution.py:91
  23.6 0.0 collective-permute-done.2
  23.7 2.1 %collective-permute-start.3 = (f32[32,512]{1,0:T(8,128)S(1)}, f32[32,512]{1,0:T(8,128)S(1)}, u32[]{:S(2)}, u32[]{:S(2)}) collective-permute-start(f32[32,512]{1,0:T(8,128)S(1)} %get-tuple-element.16), channel_id=1, source_target_pairs={{0,2},{1,9},{2,0},{3,11},{4,6},{5,13},{6,4},{7,15},{8,10},{9,1},{1... | collective-permute-start | bytes 196616 | tf_op jit(solution)/shard_map/ppermute | solution.py:91
  25.7 0.1 copy.25.refs_5_
  25.8 0.0 collective-permute-done.7.refs_2_
  25.8 2.3 %collective-permute-done.8.refs_3_ = f32[32,512]{1,0:T(8,128)S(1)} collective-permute-done((f32[32,512]{1,0:T(8,128)S(1)}, f32[32,512]{1,0:T(8,128)S(1)}, u32[]{:S(2)}, u32[]{:S(2)}) %collective-permute-start.8) | collective-permute-done | bytes 65568 | tf_op jit(solution)/shard_map/ppermute | solution.py:91
  28.1 0.0 collective-permute-done.3.refs_1_
  28.1 0.0 copy-done
  28.1 0.0 copy-done.1
  28.1 0.2 shard_map.87
  28.4 11.8 %all_to_all.11 = f32[32,1,128]{2,1,0:T(1,128)S(1)} all-to-all(f32[32,1,128]{2,1,0:T(1,128)S(1)} %bitcast.45), channel_id=1, replica_groups=mesh['wide'=16,'narrow'=2] {'wide','narrow'}, dimensions={0} | all-to-all | bytes 32768 | tf_op jit(solution)/shard_map/all_to_all | solution.py:174
  40.1 0.6 %shard_map.88 = (f32[1,1]{1,0:T(1,128)}, f32[32,512]{1,0:T(8,128)}) custom-call(f32[32,128]{1,0:T(8,128)S(1)} %bitcast.44, f32[32,512]{1,0:T(8,128)S(1)} %get-tuple-element.7.update_ref), custom_call_target="tpu_custom_call" | custom-call | tf_op jit(solution)/shard_map/pallas_call | solution.py:175
  (14 shorter events, 0.3 us)
Async XLA Ops:
  3.2 2.7 %copy-start.3 = (s32[32,2]{0,1:T(2,128)S(1)}, s32[32,2]{0,1:T(2,128)}, u32[]{:S(2)}) copy-start(s32[32,2]{0,1:T(2,128)} %param.10) | copy-start | bytes 772
  3.2 4.1 %collective-permute-start.4 = (f32[2,4,32,512]{3,2,1,0:T(8,128)S(1)}, f32[2,4,32,512]{3,2,1,0:T(8,128)S(1)}, u32[]{:S(2)}, u32[]{:S(2)}) collective-permute-start(f32[2,4,32,512]{3,2,1,0:T(8,128)S(1)} %slice_bitcast_fusion), channel_id=1, source_target_pairs={{0,1},{1,0},{2,3},{3,2},{4,5},{5,4},{6,7},{7,6},{8,9},{9,8},{10,11... | collective-permute-start | bytes 1572872 | tf_op jit(solution)/shard_map/ppermute | solution.py:121
  5.8 3.0 %collective-permute-start = (f32[2,4,32,512]{3,2,1,0:T(8,128)S(1)}, f32[2,4,32,512]{3,2,1,0:T(8,128)S(1)}, u32[]{:S(2)}, u32[]{:S(2)}) collective-permute-start(f32[2,4,32,512]{3,2,1,0:T(8,128)S(1)} %slice_bitcast_fusion.2), channel_id=1, source_target_pairs={{0,1},{1,0},{2,3},{3,2},{4,5},{5,4},{6,7},{7,6},{8,9},{9,8},{10,11... | collective-permute-start | bytes 1572872 | tf_op jit(solution)/shard_map/ppermute | solution.py:121
  5.9 4.7 %copy-start.2 = (f32[576]{0:T(1024)S(1)}, f32[576]{0:T(1024)}, u32[]{:S(2)}) copy-start(f32[576]{0:T(1024)} %param.11) | copy-start | bytes 6916
  7.4 6.4 %collective-permute-start.5 = (f32[2,2,32,512]{3,2,1,0:T(8,128)S(1)}, f32[2,2,32,512]{3,2,1,0:T(8,128)S(1)}, u32[]{:S(2)}, u32[]{:S(2)}) collective-permute-start(f32[2,2,32,512]{3,2,1,0:T(8,128)S(1)} %slice.101), channel_id=1, source_target_pairs={{0,2},{1,5},{2,0},{3,7},{4,6},{5,1},{6,4},{7,3},{8,10},{9,13},{10,... | collective-permute-start | bytes 786440 | tf_op jit(solution)/shard_map/ppermute | solution.py:91
  8.9 19.2 %copy-start = (f32[32,512]{1,0:T(8,128)S(1)}, f32[32,512]{1,0:T(8,128)}, u32[]{:S(2)}) copy-start(f32[32,512]{1,0:T(8,128)} %refs_4_.1) | copy-start | bytes 196612
  8.9 19.2 %copy-start.1 = (f32[512]{0:T(512)S(1)}, f32[512]{0:T(512)}, u32[]{:S(2)}) copy-start(f32[512]{0:T(512)} %param.12) | copy-start | bytes 6148
  9.0 6.4 %collective-permute-start.1 = (f32[2,2,32,512]{3,2,1,0:T(8,128)S(1)}, f32[2,2,32,512]{3,2,1,0:T(8,128)S(1)}, u32[]{:S(2)}, u32[]{:S(2)}) collective-permute-start(f32[2,2,32,512]{3,2,1,0:T(8,128)S(1)} %slice.92), channel_id=1, source_target_pairs={{0,8},{1,5},{2,10},{3,7},{4,12},{5,1},{6,14},{7,3},{8,0},{9,13},{1... | collective-permute-start | bytes 786440 | tf_op jit(solution)/shard_map/ppermute | solution.py:91
  13.9 5.0 %collective-permute-start.6 = (f32[2,1,32,512]{3,2,1,0:T(8,128)S(1)}, f32[2,1,32,512]{3,2,1,0:T(8,128)S(1)}, u32[]{:S(2)}, u32[]{:S(2)}) collective-permute-start(f32[2,1,32,512]{3,2,1,0:T(8,128)S(1)} %slice.103), channel_id=1, source_target_pairs={{0,4},{1,3},{2,6},{3,1},{4,0},{5,7},{6,2},{7,5},{8,12},{9,11},{10,... | collective-permute-start | bytes 393224 | tf_op jit(solution)/shard_map/ppermute | solution.py:91
  15.5 8.2 %collective-permute-start.2 = (f32[2,1,32,512]{3,2,1,0:T(8,128)S(1)}, f32[2,1,32,512]{3,2,1,0:T(8,128)S(1)}, u32[]{:S(2)}, u32[]{:S(2)}) collective-permute-start(f32[2,1,32,512]{3,2,1,0:T(8,128)S(1)} %slice.94), channel_id=1, source_target_pairs={{0,4},{1,3},{2,6},{3,1},{4,0},{5,7},{6,2},{7,5},{8,12},{9,11},{10,... | collective-permute-start | bytes 393224 | tf_op jit(solution)/shard_map/ppermute | solution.py:91
  19.0 6.8 %collective-permute-start.7 = (f32[32,512]{1,0:T(8,128)S(1)}, f32[32,512]{1,0:T(8,128)S(1)}, u32[]{:S(2)}, u32[]{:S(2)}) collective-permute-start(f32[32,512]{1,0:T(8,128)S(1)} %get-tuple-element.15), channel_id=1, source_target_pairs={{0,16},{1,17},{2,18},{3,19},{4,20},{5,21},{6,22},{7,23},{8,24},{9,... | collective-permute-start | bytes 196616 | tf_op jit(solution)/shard_map/ppermute | solution.py:91
  22.0 6.2 %collective-permute-start.8 = (f32[32,512]{1,0:T(8,128)S(1)}, f32[32,512]{1,0:T(8,128)S(1)}, u32[]{:S(2)}, u32[]{:S(2)}) collective-permute-start(f32[32,512]{1,0:T(8,128)S(1)} %get-tuple-element.14), channel_id=1, source_target_pairs={{0,24},{1,25},{2,26},{3,27},{4,28},{5,29},{6,30},{7,31},{8,16},{9,... | collective-permute-start | bytes 196616 | tf_op jit(solution)/shard_map/ppermute | solution.py:91
  23.7 4.5 %collective-permute-start.3 = (f32[32,512]{1,0:T(8,128)S(1)}, f32[32,512]{1,0:T(8,128)S(1)}, u32[]{:S(2)}, u32[]{:S(2)}) collective-permute-start(f32[32,512]{1,0:T(8,128)S(1)} %get-tuple-element.16), channel_id=1, source_target_pairs={{0,2},{1,9},{2,0},{3,11},{4,6},{5,13},{6,4},{7,15},{8,10},{9,1},{1... | collective-permute-start | bytes 196616 | tf_op jit(solution)/shard_map/ppermute | solution.py:91

commit v7 on v6

--- a/solution.py
+++ b/solution.py
@@ -80,10 +80,12 @@
     square_ref[...] = jnp.full(square_ref.shape, jnp.sum(update * update))
 
 
-def norm_kernel(entries, squares_ref, update_ref, norm_ref, out_ref):
-    out_ref[...] = update_ref[...]
+def norm_kernel(entries, squares_ref, update_ref, norm_ref, out_ref, out_sem):
+    copy = pltpu.make_async_copy(update_ref, out_ref, out_sem)
+    copy.start()
     total = jnp.sum(squares_ref[...], axis=0, keepdims=True)
     norm_ref[...] = jnp.sqrt(total / entries)[:, :1]
+    copy.wait()
 
 
 def flip(value, devices, masks):
@@ -178,6 +180,8 @@
                 jax.ShapeDtypeStruct((1, 1), jnp.float32),
                 jax.ShapeDtypeStruct(other_terms.shape, jnp.float32),
             ],
+            out_specs=[pl.BlockSpec(memory_space=pltpu.VMEM), pl.BlockSpec(memory_space=pltpu.HBM)],
+            scratch_shapes=[pltpu.SemaphoreType.DMA],
             compiler_params=pltpu.CompilerParams(vmem_limit_bytes=4 << 20),
         )(squares, update)
         update_norm = update_norm.reshape(())

time: 40.3 us -> 40.8 us (1.012); the launches traced: 40.8 us -> 40.3 us
  blocking collectives: 11.8 us -> 10.2 us
  Pallas kernels: 2.57 us -> 3.58 us
  waiting for transfers between devices: 9.62 us -> 10.5 us
  starting transfers between devices: 14.5 us -> 13.7 us
    ppermute x2, starting transfers between devices: 2.63 us -> 0.63 us  [fast_ladder(): pieces = [s[:, 0] + lax.ppermute(s[:, 1], AXES, swap) for s in pieces]]
    all_to_all x1, blocking collectives: 11.8 us -> 10.2 us  [shards(): squares = lax.all_to_all(squares, AXES, 0, 0, tiled=True)]
    ppermute x7, starting transfers between devices: 11.8 us -> 13.1 us  [flip(): return lax.ppermute(value, AXES, pairs)]
    ppermute x7, waiting for transfers between devices: 8.23 us -> 9.22 us  [flip(): return lax.ppermute(value, AXES, pairs)]
    pallas_call x1, Pallas kernels: 0.64 us -> 1.15 us  [shards(): pl.pallas_call(functools.partial(norm_kernel, rows * width), out_shape=[j...]
    pallas_call x1, Pallas kernels: 1.72 us -> 2.23 us  [fast_ladder(): pl.pallas_call(functools.partial(ladder_kernel, block_rows, wide // 4), o...]
  transfers between devices with their start and end apart: 9 -> 9, of which waited for: 5 -> 6; matrix products, arithmetic and copies ran while one was open for 2% -> 2% of each run, Pallas kernels for 0% -> 0%
where the time goes in v7:
time: 40.8 us; the launch traced here: 40.3 us
  starting transfers between devices  13.7 us (34%)
  waiting for transfers between devices  10.5 us (26%)
  blocking collectives  10.2 us (25%)
  Pallas kernels  3.58 us (9%)
  between operations  1.43 us (4%)
  other arithmetic  0.47 us (1%)
  local copies, waits for them, and re-layouts  0.44 us (1%)
    ppermute x7, starting transfers between devices, flip(): return lax.ppermute(value, AXES, pairs)  13.1 us
    all_to_all x1, blocking collectives, shards(): squares = lax.all_to_all(squares, AXES, 0, 0, tiled=True)  10.2 us
    ppermute x7, waiting for transfers between devices, flip(): return lax.ppermute(value, AXES, pairs)  9.22 us
    pallas_call x1, Pallas kernels, fast_ladder(): pl.pallas_call(functools.partial(ladder_kernel, block_rows, wide // 4), o...  2.23 us
    ppermute x2, waiting for transfers between devices, fast_ladder(): pieces = [s[:, 0] + lax.ppermute(s[:, 1], AXES, swap) for s in pieces]  1.29 us
    pallas_call x1, Pallas kernels, shards(): pl.pallas_call(functools.partial(norm_kernel, rows * width), out_shape=[j...  1.15 us
  transfers between devices with their start and end apart: 9, of which 6 were waited for; matrix products, arithmetic and copies ran while one was open for 2% of the time, Pallas kernels for 0%

profile of v7, /device:TPU:0, one launch (start us, length us, event | category | flops | bytes accessed | tf_op | source)
XLA Modules:
  0.0 40.3 jit_solution(4554144412051077482)
XLA Ops:
  1.3 2.2 %shard_map.86 = f32[1024,512]{1,0:T(8,128)S(1)} custom-call(s32[1]{0:T(128)S(6)} %copy.31.count_ref, bf16[6,256,1024]{2,1,0:T(8,128)(2,1)} %bitcast.51, bf16[6,256,512]{2,1,0:T(8,128)(2,1)} %bitcast.52), custom_call_target="tpu_custom_call" | custom-call | tf_op jit(solution)/shard_map/pallas_call | solution.py:101
  3.5 0.2 fusion.2
  3.7 0.0 copy-start.3
  3.7 0.1 collective-permute-start.4
  3.9 0.6 %collective-permute-start = (f32[2,4,32,512]{3,2,1,0:T(8,128)S(1)}, f32[2,4,32,512]{3,2,1,0:T(8,128)S(1)}, u32[]{:S(2)}, u32[]{:S(2)}) collective-permute-start(f32[2,4,32,512]{3,2,1,0:T(8,128)S(1)} %slice_bitcast_fusion.2), channel_id=1, source_target_pairs={{0,1},{1,0},{2,3},{3,2},{4,5},{5,4},{6,7},{7,6},{8,9},{9,8},{10,11... | collective-permute-start | bytes 1572872 | tf_op jit(solution)/shard_map/ppermute | solution.py:123
  4.4 0.0 copy-done.3
  4.4 0.0 copy-start.2
  4.4 1.3 %collective-permute-done.4 = f32[2,4,32,512]{3,2,1,0:T(8,128)S(1)} collective-permute-done((f32[2,4,32,512]{3,2,1,0:T(8,128)S(1)}, f32[2,4,32,512]{3,2,1,0:T(8,128)S(1)}, u32[]{:S(2)}, u32[]{:S(2)}) %collective-permute-start.4) | collective-permute-done | bytes 524320 | tf_op jit(solution)/shard_map/ppermute | solution.py:123
  5.7 0.1 fusion
  5.8 4.5 %collective-permute-start.5 = (f32[2,2,32,512]{3,2,1,0:T(8,128)S(1)}, f32[2,2,32,512]{3,2,1,0:T(8,128)S(1)}, u32[]{:S(2)}, u32[]{:S(2)}) collective-permute-start(f32[2,2,32,512]{3,2,1,0:T(8,128)S(1)} %slice.101), channel_id=1, source_target_pairs={{0,2},{1,5},{2,0},{3,7},{4,6},{5,1},{6,4},{7,3},{8,10},{9,13},{10,... | collective-permute-start | bytes 786440 | tf_op jit(solution)/shard_map/ppermute | solution.py:93
  10.4 0.0 collective-permute-done
  10.4 0.1 fusion.1
  10.5 0.0 copy-start
  10.5 0.0 copy-start.1
  10.5 1.6 %collective-permute-start.1 = (f32[2,2,32,512]{3,2,1,0:T(8,128)S(1)}, f32[2,2,32,512]{3,2,1,0:T(8,128)S(1)}, u32[]{:S(2)}, u32[]{:S(2)}) collective-permute-start(f32[2,2,32,512]{3,2,1,0:T(8,128)S(1)} %slice.92), channel_id=1, source_target_pairs={{0,8},{1,5},{2,10},{3,7},{4,12},{5,1},{6,14},{7,3},{8,0},{9,13},{1... | collective-permute-start | bytes 786440 | tf_op jit(solution)/shard_map/ppermute | solution.py:93
  12.1 0.0 copy-done.2
  12.2 0.2 select_reduce_fusion
  12.3 2.4 %collective-permute-done.5 = f32[2,2,32,512]{3,2,1,0:T(8,128)S(1)} collective-permute-done((f32[2,2,32,512]{3,2,1,0:T(8,128)S(1)}, f32[2,2,32,512]{3,2,1,0:T(8,128)S(1)}, u32[]{:S(2)}, u32[]{:S(2)}) %collective-permute-start.5) | collective-permute-done | bytes 262176 | tf_op jit(solution)/shard_map/ppermute | solution.py:93
  14.8 0.6 %collective-permute-start.6 = (f32[2,1,32,512]{3,2,1,0:T(8,128)S(1)}, f32[2,1,32,512]{3,2,1,0:T(8,128)S(1)}, u32[]{:S(2)}, u32[]{:S(2)}) collective-permute-start(f32[2,1,32,512]{3,2,1,0:T(8,128)S(1)} %slice.103), channel_id=1, source_target_pairs={{0,4},{1,3},{2,6},{3,1},{4,0},{5,7},{6,2},{7,5},{8,12},{9,11},{10,... | collective-permute-start | bytes 393224 | tf_op jit(solution)/shard_map/ppermute | solution.py:93
  15.4 1.6 %collective-permute-done.1 = f32[2,2,32,512]{3,2,1,0:T(8,128)S(1)} collective-permute-done((f32[2,2,32,512]{3,2,1,0:T(8,128)S(1)}, f32[2,2,32,512]{3,2,1,0:T(8,128)S(1)}, u32[]{:S(2)}, u32[]{:S(2)}) %collective-permute-start.1) | collective-permute-done | bytes 262176 | tf_op jit(solution)/shard_map/ppermute | solution.py:93
  17.0 0.2 collective-permute-start.2
  17.2 2.6 %collective-permute-done.6 = f32[2,1,32,512]{3,2,1,0:T(8,128)S(1)} collective-permute-done((f32[2,1,32,512]{3,2,1,0:T(8,128)S(1)}, f32[2,1,32,512]{3,2,1,0:T(8,128)S(1)}, u32[]{:S(2)}, u32[]{:S(2)}) %collective-permute-start.6) | collective-permute-done | bytes 131104 | tf_op jit(solution)/shard_map/ppermute | solution.py:93
  19.8 1.7 %collective-permute-start.7 = (f32[32,512]{1,0:T(8,128)S(1)}, f32[32,512]{1,0:T(8,128)S(1)}, u32[]{:S(2)}, u32[]{:S(2)}) collective-permute-start(f32[32,512]{1,0:T(8,128)S(1)} %get-tuple-element.15), channel_id=1, source_target_pairs={{0,16},{1,17},{2,18},{3,19},{4,20},{5,21},{6,22},{7,23},{8,24},{9,... | collective-permute-start | bytes 196616 | tf_op jit(solution)/shard_map/ppermute | solution.py:93
  21.5 2.9 %collective-permute-start.8 = (f32[32,512]{1,0:T(8,128)S(1)}, f32[32,512]{1,0:T(8,128)S(1)}, u32[]{:S(2)}, u32[]{:S(2)}) collective-permute-start(f32[32,512]{1,0:T(8,128)S(1)} %get-tuple-element.14), channel_id=1, source_target_pairs={{0,24},{1,25},{2,26},{3,27},{4,28},{5,29},{6,30},{7,31},{8,16},{9,... | collective-permute-start | bytes 196616 | tf_op jit(solution)/shard_map/ppermute | solution.py:93
  24.4 0.0 collective-permute-done.2
  24.4 1.6 %collective-permute-start.3 = (f32[32,512]{1,0:T(8,128)S(1)}, f32[32,512]{1,0:T(8,128)S(1)}, u32[]{:S(2)}, u32[]{:S(2)}) collective-permute-start(f32[32,512]{1,0:T(8,128)S(1)} %get-tuple-element.16), channel_id=1, source_target_pairs={{0,2},{1,9},{2,0},{3,11},{4,6},{5,13},{6,4},{7,15},{8,10},{9,1},{1... | collective-permute-start | bytes 196616 | tf_op jit(solution)/shard_map/ppermute | solution.py:93
  26.0 0.1 copy.25.refs_5_
  26.1 0.0 collective-permute-done.7.refs_2_
  26.1 1.9 %collective-permute-done.8.refs_3_ = f32[32,512]{1,0:T(8,128)S(1)} collective-permute-done((f32[32,512]{1,0:T(8,128)S(1)}, f32[32,512]{1,0:T(8,128)S(1)}, u32[]{:S(2)}, u32[]{:S(2)}) %collective-permute-start.8) | collective-permute-done | bytes 65568 | tf_op jit(solution)/shard_map/ppermute | solution.py:93
  28.0 0.8 %collective-permute-done.3.refs_1_ = f32[32,512]{1,0:T(8,128)S(1)} collective-permute-done((f32[32,512]{1,0:T(8,128)S(1)}, f32[32,512]{1,0:T(8,128)S(1)}, u32[]{:S(2)}, u32[]{:S(2)}) %collective-permute-start.3) | collective-permute-done | bytes 65568 | tf_op jit(solution)/shard_map/ppermute | solution.py:93
  28.8 0.0 copy-done
  28.8 0.0 copy-done.1
  28.8 0.2 shard_map.87
  29.0 10.2 %all_to_all.11 = f32[32,1,128]{2,1,0:T(1,128)S(1)} all-to-all(f32[32,1,128]{2,1,0:T(1,128)S(1)} %bitcast.45), channel_id=1, replica_groups=mesh['wide'=16,'narrow'=2] {'wide','narrow'}, dimensions={0} | all-to-all | bytes 32768 | tf_op jit(solution)/shard_map/all_to_all | solution.py:176
  39.1 1.1 %shard_map.88 = (f32[1,1]{1,0:T(1,128)}, f32[32,512]{1,0:T(8,128)}) custom-call(f32[32,128]{1,0:T(8,128)S(1)} %bitcast.44, f32[32,512]{1,0:T(8,128)S(1)} %get-tuple-element.7.update_ref), custom_call_target="tpu_custom_call" | custom-call | tf_op jit(solution)/shard_map/pallas_call | solution.py:177
  (14 shorter events, 0.3 us)
Async XLA Ops:
  3.7 0.7 %copy-start.3 = (s32[32,2]{0,1:T(2,128)S(1)}, s32[32,2]{0,1:T(2,128)}, u32[]{:S(2)}) copy-start(s32[32,2]{0,1:T(2,128)} %param.10) | copy-start | bytes 772
  3.7 2.0 %collective-permute-start.4 = (f32[2,4,32,512]{3,2,1,0:T(8,128)S(1)}, f32[2,4,32,512]{3,2,1,0:T(8,128)S(1)}, u32[]{:S(2)}, u32[]{:S(2)}) collective-permute-start(f32[2,4,32,512]{3,2,1,0:T(8,128)S(1)} %slice_bitcast_fusion), channel_id=1, source_target_pairs={{0,1},{1,0},{2,3},{3,2},{4,5},{5,4},{6,7},{7,6},{8,9},{9,8},{10,11... | collective-permute-start | bytes 1572872 | tf_op jit(solution)/shard_map/ppermute | solution.py:123
  3.9 6.5 %collective-permute-start = (f32[2,4,32,512]{3,2,1,0:T(8,128)S(1)}, f32[2,4,32,512]{3,2,1,0:T(8,128)S(1)}, u32[]{:S(2)}, u32[]{:S(2)}) collective-permute-start(f32[2,4,32,512]{3,2,1,0:T(8,128)S(1)} %slice_bitcast_fusion.2), channel_id=1, source_target_pairs={{0,1},{1,0},{2,3},{3,2},{4,5},{5,4},{6,7},{7,6},{8,9},{9,8},{10,11... | collective-permute-start | bytes 1572872 | tf_op jit(solution)/shard_map/ppermute | solution.py:123
  4.4 7.7 %copy-start.2 = (f32[576]{0:T(1024)S(1)}, f32[576]{0:T(1024)}, u32[]{:S(2)}) copy-start(f32[576]{0:T(1024)} %param.11) | copy-start | bytes 6916
  5.8 8.9 %collective-permute-start.5 = (f32[2,2,32,512]{3,2,1,0:T(8,128)S(1)}, f32[2,2,32,512]{3,2,1,0:T(8,128)S(1)}, u32[]{:S(2)}, u32[]{:S(2)}) collective-permute-start(f32[2,2,32,512]{3,2,1,0:T(8,128)S(1)} %slice.101), channel_id=1, source_target_pairs={{0,2},{1,5},{2,0},{3,7},{4,6},{5,1},{6,4},{7,3},{8,10},{9,13},{10,... | collective-permute-start | bytes 786440 | tf_op jit(solution)/shard_map/ppermute | solution.py:93
  10.5 18.3 %copy-start = (f32[32,512]{1,0:T(8,128)S(1)}, f32[32,512]{1,0:T(8,128)}, u32[]{:S(2)}) copy-start(f32[32,512]{1,0:T(8,128)} %refs_4_.1) | copy-start | bytes 196612
  10.5 18.3 %copy-start.1 = (f32[512]{0:T(512)S(1)}, f32[512]{0:T(512)}, u32[]{:S(2)}) copy-start(f32[512]{0:T(512)} %param.12) | copy-start | bytes 6148
  10.5 6.4 %collective-permute-start.1 = (f32[2,2,32,512]{3,2,1,0:T(8,128)S(1)}, f32[2,2,32,512]{3,2,1,0:T(8,128)S(1)}, u32[]{:S(2)}, u32[]{:S(2)}) collective-permute-start(f32[2,2,32,512]{3,2,1,0:T(8,128)S(1)} %slice.92), channel_id=1, source_target_pairs={{0,8},{1,5},{2,10},{3,7},{4,12},{5,1},{6,14},{7,3},{8,0},{9,13},{1... | collective-permute-start | bytes 786440 | tf_op jit(solution)/shard_map/ppermute | solution.py:93
  14.8 5.0 %collective-permute-start.6 = (f32[2,1,32,512]{3,2,1,0:T(8,128)S(1)}, f32[2,1,32,512]{3,2,1,0:T(8,128)S(1)}, u32[]{:S(2)}, u32[]{:S(2)}) collective-permute-start(f32[2,1,32,512]{3,2,1,0:T(8,128)S(1)} %slice.103), channel_id=1, source_target_pairs={{0,4},{1,3},{2,6},{3,1},{4,0},{5,7},{6,2},{7,5},{8,12},{9,11},{10,... | collective-permute-start | bytes 393224 | tf_op jit(solution)/shard_map/ppermute | solution.py:93
  17.0 7.4 %collective-permute-start.2 = (f32[2,1,32,512]{3,2,1,0:T(8,128)S(1)}, f32[2,1,32,512]{3,2,1,0:T(8,128)S(1)}, u32[]{:S(2)}, u32[]{:S(2)}) collective-permute-start(f32[2,1,32,512]{3,2,1,0:T(8,128)S(1)} %slice.94), channel_id=1, source_target_pairs={{0,4},{1,3},{2,6},{3,1},{4,0},{5,7},{6,2},{7,5},{8,12},{9,11},{10,... | collective-permute-start | bytes 393224 | tf_op jit(solution)/shard_map/ppermute | solution.py:93
  19.8 6.2 %collective-permute-start.7 = (f32[32,512]{1,0:T(8,128)S(1)}, f32[32,512]{1,0:T(8,128)S(1)}, u32[]{:S(2)}, u32[]{:S(2)}) collective-permute-start(f32[32,512]{1,0:T(8,128)S(1)} %get-tuple-element.15), channel_id=1, source_target_pairs={{0,16},{1,17},{2,18},{3,19},{4,20},{5,21},{6,22},{7,23},{8,24},{9,... | collective-permute-start | bytes 196616 | tf_op jit(solution)/shard_map/ppermute | solution.py:93
  21.5 6.5 %collective-permute-start.8 = (f32[32,512]{1,0:T(8,128)S(1)}, f32[32,512]{1,0:T(8,128)S(1)}, u32[]{:S(2)}, u32[]{:S(2)}) collective-permute-start(f32[32,512]{1,0:T(8,128)S(1)} %get-tuple-element.14), channel_id=1, source_target_pairs={{0,24},{1,25},{2,26},{3,27},{4,28},{5,29},{6,30},{7,31},{8,16},{9,... | collective-permute-start | bytes 196616 | tf_op jit(solution)/shard_map/ppermute | solution.py:93
  24.4 4.3 %collective-permute-start.3 = (f32[32,512]{1,0:T(8,128)S(1)}, f32[32,512]{1,0:T(8,128)S(1)}, u32[]{:S(2)}, u32[]{:S(2)}) collective-permute-start(f32[32,512]{1,0:T(8,128)S(1)} %get-tuple-element.16), channel_id=1, source_target_pairs={{0,2},{1,9},{2,0},{3,11},{4,6},{5,13},{6,4},{7,15},{8,10},{9,1},{1... | collective-permute-start | bytes 196616 | tf_op jit(solution)/shard_map/ppermute | solution.py:93
